TPU v7x, 512 devices: a whole 4x4x16 slice. The times are simulated.
512 devices in a mesh: ctx: 32 (over x, z_lo), tp: 16 (over z_hi, y, core).
Axes of the slice: x: 4, y: 4, z: 16 (z_hi: 2, z_lo: 8; z = z_hi * 8 + z_lo), core: 2. Of those that a mesh axis runs over, the one named last changes fastest.
Arguments:
- out_grad: bfloat16 [4096, 4096], P('ctx', 'tp'), may hold values from -6 to 6
- out_proj: bfloat16 [4096, 4096], P(None, 'tp'), may hold values from -0.09375 to 0.09375
- queries: bfloat16 [4096, 4096], P('ctx', 'tp'), may hold values from -6 to 6
- keys: bfloat16 [4096, 4096], P('ctx', 'tp'), may hold values from -6 to 6
- values: bfloat16 [4096, 4096], P('ctx', 'tp'), may hold values from -6 to 6
- conv_out: bfloat16 [4096, 4096], P('ctx', 'tp'), may hold values from -6 to 6
- long_filter: float32 [4096, 4096], P('ctx', 'tp'), may hold values from -6 to 6
- skip_gain: float32 [4096], P('tp'), may hold values from 0.5 to 2
Outputs:
- grad_q: bfloat16 [4096, 4096], P('ctx', 'tp')
- grad_k: bfloat16 [4096, 4096], P('ctx', 'tp')
- grad_v: bfloat16 [4096, 4096], P('ctx', 'tp')
- filter_grad: float32 [4096, 4096], P('ctx', 'tp')
All inputs are finite; a program needn't handle non-finite values.
Results may differ from a plain program's by a relative error of at most 0.0011.
Values may be sent and summed in bfloat16 or wider, within the bound.
No kernel may reach another device: no remote copies, remote signals or barrier semaphores. Data moves between devices by JAX's collectives and lax.ppermute only.
A program may use at most 64 MiB of HBM per device.

v0:
```python
import math

import jax
import jax.numpy as jnp
from jax import lax
from jax.sharding import PartitionSpec as P


def from_partner(x, axis, apart):
    return lax.ppermute(x, axis, [(i, i ^ 1 << apart) for i in range(lax.axis_size(axis))])


def phase(numer, denom, factor):
    turns = numer.astype(jnp.float32) * (factor * math.pi / denom)
    return (jnp.cos(turns), jnp.sin(turns))


def rotate(real_part, imag_part, cos_w, sin_w):
    return (real_part * cos_w - imag_part * sin_w, real_part * sin_w + imag_part * cos_w)


def local_dft(real_part, imag_part, sign_value):
    length = real_part.shape[2]
    index = jnp.arange(length, dtype=jnp.int32)
    cos_table, sin_table = phase(index[:, None] * index[None, :] % length, length, 2.0 * sign_value)

    def apply_table(table, data):
        return jnp.einsum("kr,ferc->fekc", table, data, precision=lax.Precision.HIGHEST)

    out_real = apply_table(cos_table, real_part) - apply_table(sin_table, imag_part)
    out_imag = apply_table(cos_table, imag_part) + apply_table(sin_table, real_part)
    return (out_real, out_imag)


def reverse_bits(device_pos, levels):
    result = jnp.zeros((), jnp.int32)
    for step in range(levels):
        result = result | (device_pos >> step & 1) << levels - 1 - step
    return result


def twist_pairs(fields, total_len):
    device_pos = lax.axis_index("ctx")
    stacked = jnp.stack(fields)
    shard_len = stacked.shape[1]
    positions = device_pos * shard_len + jnp.arange(shard_len, dtype=jnp.int32)
    cos_n, sin_n = phase(positions, total_len, -1.0)
    real_part = jnp.stack([stacked, stacked * cos_n[:, None]], axis=1)
    imag_part = jnp.stack([jnp.zeros_like(stacked), stacked * sin_n[:, None]], axis=1)
    return (real_part, imag_part)


def forward_transform(real_part, imag_part, total_len):
    shard_count = lax.axis_size("ctx")
    levels = shard_count.bit_length() - 1
    device_pos = lax.axis_index("ctx")
    num_fields, _, shard_len, channels = real_part.shape
    for step in range(levels):
        bit_pos = levels - 1 - step
        half_span = 1 << bit_pos
        other_real, other_imag = from_partner((real_part, imag_part), "ctx", bit_pos)
        upper_side = device_pos >> bit_pos & 1 == 1
        cos_w, sin_w = phase(device_pos % half_span, half_span, -1.0)
        diff_real, diff_imag = rotate(other_real - real_part, other_imag - imag_part, cos_w, sin_w)
        real_part = jnp.where(upper_side, diff_real, real_part + other_real)
        imag_part = jnp.where(upper_side, diff_imag, imag_part + other_imag)
    freq_value = reverse_bits(device_pos, levels)
    row_index = jnp.arange(shard_len, dtype=jnp.int32)
    cos_w, sin_w = phase(row_index * freq_value % total_len, total_len, -2.0)
    real_part, imag_part = rotate(
        real_part, imag_part, cos_w[None, None, :, None], sin_w[None, None, :, None]
    )
    return local_dft(real_part, imag_part, -1.0)


def inverse_transform(real_part, imag_part, total_len):
    shard_count = lax.axis_size("ctx")
    levels = shard_count.bit_length() - 1
    device_pos = lax.axis_index("ctx")
    num_fields, _, shard_len, channels = real_part.shape
    real_part, imag_part = local_dft(real_part, imag_part, 1.0)
    row_index = jnp.arange(shard_len, dtype=jnp.int32)
    freq_value = reverse_bits(device_pos, levels)
    cos_w, sin_w = phase(row_index * freq_value % total_len, total_len, 2.0)
    real_part, imag_part = rotate(
        real_part, imag_part, cos_w[None, None, :, None], sin_w[None, None, :, None]
    )
    for bit_pos in range(levels):
        half_span = 1 << bit_pos
        other_real, other_imag = from_partner((real_part, imag_part), "ctx", bit_pos)
        upper_side = device_pos >> bit_pos & 1 == 1
        cos_w, sin_w = phase(device_pos % half_span, half_span, 1.0)
        self_real, self_imag = rotate(real_part, imag_part, cos_w, sin_w)
        peer_real, peer_imag = rotate(other_real, other_imag, cos_w, sin_w)
        real_part, imag_part = (
            jnp.where(upper_side, other_real - self_real, real_part + peer_real),
            jnp.where(upper_side, other_imag - self_imag, imag_part + peer_imag),
        )
    positions = device_pos * shard_len + row_index
    cos_n, sin_n = phase(positions, total_len, 1.0)
    combined = (
        real_part[:, 0]
        + cos_n[None, :, None] * real_part[:, 1]
        - sin_n[None, :, None] * imag_part[:, 1]
    )
    return combined * (1.0 / (2.0 * total_len))


def body(out_grad, out_proj, queries, keys, values, conv_out, long_filter, skip_gain):
    tok_rows, channels = queries.shape
    shard_count = lax.axis_size("ctx")
    total_len = tok_rows * shard_count
    key_float = keys.astype(jnp.float32)
    value_float = values.astype(jnp.float32)
    gated_in = key_float * value_float
    inv_root = 1.0 / math.sqrt(total_len)
    scaled_filter = long_filter * inv_root
    pair_real, pair_imag = twist_pairs([scaled_filter, gated_in], total_len)
    first_real, first_imag = forward_transform(pair_real, pair_imag, total_len)
    act_grad = jnp.dot(
        lax.all_gather(out_grad, "tp", axis=1, tiled=True),
        out_proj,
        preferred_element_type=jnp.float32,
    )
    gated_grad = act_grad * queries.astype(jnp.float32)
    single_real, single_imag = twist_pairs([gated_grad], total_len)
    second_real, second_imag = forward_transform(single_real, single_imag, total_len)
    filter_real, filter_imag = (first_real[0], first_imag[0])
    gated_real, gated_imag = (first_real[1], first_imag[1])
    grad_real, grad_imag = (second_real[0], second_imag[0])
    corr_real = jnp.stack(
        [
            filter_real * grad_real + filter_imag * grad_imag,
            gated_real * grad_real + gated_imag * grad_imag,
        ]
    )
    corr_imag = jnp.stack(
        [
            filter_real * grad_imag - filter_imag * grad_real,
            gated_real * grad_imag - gated_imag * grad_real,
        ]
    )
    results = inverse_transform(corr_real, corr_imag, total_len)
    grad_q = (act_grad * conv_out.astype(jnp.float32)).astype(jnp.bfloat16)
    input_grad = results[0] + skip_gain[None, :] * gated_grad
    grad_k = (input_grad * value_float).astype(jnp.bfloat16)
    grad_v = (input_grad * key_float).astype(jnp.bfloat16)
    filter_grad = results[1] * inv_root
    return (grad_q, grad_k, grad_v, filter_grad)


def solution(mesh):
    return jax.shard_map(
        body,
        mesh=mesh,
        in_specs=(
            P("ctx", "tp"),
            P(None, "tp"),
            P("ctx", "tp"),
            P("ctx", "tp"),
            P("ctx", "tp"),
            P("ctx", "tp"),
            P("ctx", "tp"),
            P("tp"),
        ),
        out_specs=(P("ctx", "tp"), P("ctx", "tp"), P("ctx", "tp"), P("ctx", "tp")),
        check_vma=False,
    )
```

profile of v0, /device:TPU:6, one launch (start us, length us, event | category | flops | bytes accessed | tf_op | source)
XLA Modules:
  0.0 580.7 jit_solution(13866660558568756837)
XLA Ops:
  12.8 4.0 collective-permute-start.1
  17.0 9.9 %collective-permute-done = f32[2,2,128,256]{3,2,1,0:T(8,128)} collective-permute-done((f32[2,2,128,256]{3,2,1,0:T(8,128)S(1)}, f32[2,2,128,256]{3,2,1,0:T(8,128)}, u32[]{:S(2)}, u32[]{:S(2)}) %collective-permute-start) | collective-permute-done | bytes 524320 | tf_op jit(solution)/shard_map/ppermute | solution.py:10
  26.9 10.1 %collective-permute-done.1 = f32[2,2,128,256]{3,2,1,0:T(8,128)} collective-permute-done((f32[2,2,128,256]{3,2,1,0:T(8,128)}, f32[2,2,128,256]{3,2,1,0:T(8,128)}, u32[]{:S(2)}, u32[]{:S(2)}) %collective-permute-start.1) | collective-permute-done | bytes 524320 | tf_op jit(solution)/shard_map/ppermute | solution.py:10
  45.2 10.7 %collective-permute-done.2 = f32[2,2,128,256]{3,2,1,0:T(8,128)S(1)} collective-permute-done((f32[2,2,128,256]{3,2,1,0:T(8,128)S(1)}, f32[2,2,128,256]{3,2,1,0:T(8,128)S(1)}, u32[]{:S(2)}, u32[]{:S(2)}) %collective-permute-start.2) | collective-permute-done | bytes 524320 | tf_op jit(solution)/shard_map/ppermute | solution.py:10
  56.8 8.5 %collective-permute-done.3 = f32[2,2,128,256]{3,2,1,0:T(8,128)} collective-permute-done((f32[2,2,128,256]{3,2,1,0:T(8,128)}, f32[2,2,128,256]{3,2,1,0:T(8,128)}, u32[]{:S(2)}, u32[]{:S(2)}) %collective-permute-start.3) | collective-permute-done | bytes 524320 | tf_op jit(solution)/shard_map/ppermute | solution.py:10
  67.1 9.0 %collective-permute-start.4 = (f32[2,2,128,256]{3,2,1,0:T(8,128)S(1)}, f32[2,2,128,256]{3,2,1,0:T(8,128)}, u32[]{:S(2)}, u32[]{:S(2)}) collective-permute-start(f32[2,2,128,256]{3,2,1,0:T(8,128)S(1)} %get-tuple-element.18), channel_id=1, source_target_pairs={{0,64},{16,80},{32,96},{48,112},{64,0},{80,16},{96,32},{112,48},{1... | collective-permute-start | bytes 1572872 | tf_op jit(solution)/shard_map/ppermute | solution.py:10
  78.2 85.4 %collective-permute-done.4 = f32[2,2,128,256]{3,2,1,0:T(8,128)} collective-permute-done((f32[2,2,128,256]{3,2,1,0:T(8,128)S(1)}, f32[2,2,128,256]{3,2,1,0:T(8,128)}, u32[]{:S(2)}, u32[]{:S(2)}) %collective-permute-start.4) | collective-permute-done | bytes 524320 | tf_op jit(solution)/shard_map/ppermute | solution.py:10
  163.6 11.1 %collective-permute-done.5 = f32[2,2,128,256]{3,2,1,0:T(8,128)} collective-permute-done((f32[2,2,128,256]{3,2,1,0:T(8,128)S(1)}, f32[2,2,128,256]{3,2,1,0:T(8,128)}, u32[]{:S(2)}, u32[]{:S(2)}) %collective-permute-start.5) | collective-permute-done | bytes 524320 | tf_op jit(solution)/shard_map/ppermute | solution.py:10
  178.4 4.8 collective-permute-start.7
  195.5 4.7 collective-permute-done.10
  200.2 4.0 collective-permute-done.11
  212.1 8.2 %collective-permute-done.7 = f32[2,2,128,256]{3,2,1,0:T(8,128)} collective-permute-done((f32[2,2,128,256]{3,2,1,0:T(8,128)S(1)}, f32[2,2,128,256]{3,2,1,0:T(8,128)}, u32[]{:S(2)}, u32[]{:S(2)}) %collective-permute-start.7) | collective-permute-done | bytes 524320 | tf_op jit(solution)/shard_map/ppermute | solution.py:10
  230.1 8.0 %collective-permute-start.14 = (f32[1,2,128,256]{3,2,1,0:T(8,128)S(1)}, f32[1,2,128,256]{3,2,1,0:T(8,128)S(1)}, u32[]{:S(2)}, u32[]{:S(2)}) collective-permute-start(f32[1,2,128,256]{3,2,1,0:T(8,128)S(1)} %get-tuple-element.36), channel_id=1, source_target_pairs={{0,64},{16,80},{32,96},{48,112},{64,0},{80,16},{96,32},{112,48},{1... | collective-permute-start | bytes 786440 | tf_op jit(solution)/shard_map/ppermute | solution.py:10
  240.0 15.8 %collective-permute-done.9 = f32[2,2,128,256]{3,2,1,0:T(8,128)S(1)} collective-permute-done((f32[2,2,128,256]{3,2,1,0:T(8,128)}, f32[2,2,128,256]{3,2,1,0:T(8,128)S(1)}, u32[]{:S(2)}, u32[]{:S(2)}) %collective-permute-start.9) | collective-permute-done | bytes 524320 | tf_op jit(solution)/shard_map/ppermute | solution.py:10
  259.6 12.2 %collective-permute-done.15 = f32[1,2,128,256]{3,2,1,0:T(8,128)S(1)} collective-permute-done((f32[1,2,128,256]{3,2,1,0:T(8,128)S(1)}, f32[1,2,128,256]{3,2,1,0:T(8,128)S(1)}, u32[]{:S(2)}, u32[]{:S(2)}) %collective-permute-start.15) | collective-permute-done | bytes 262176 | tf_op jit(solution)/shard_map/ppermute | solution.py:10
  271.9 13.6 %collective-permute-start.16 = (f32[1,2,128,256]{3,2,1,0:T(8,128)S(1)}, f32[1,2,128,256]{3,2,1,0:T(8,128)S(1)}, u32[]{:S(2)}, u32[]{:S(2)}) collective-permute-start(f32[1,2,128,256]{3,2,1,0:T(8,128)S(1)} %get-tuple-element.34), channel_id=1, source_target_pairs={{0,32},{16,48},{32,0},{48,16},{64,96},{80,112},{96,64},{112,80},{1... | collective-permute-start | bytes 786440 | tf_op jit(solution)/shard_map/ppermute | solution.py:10
  288.7 17.0 %collective-permute-done.16 = f32[1,2,128,256]{3,2,1,0:T(8,128)S(1)} collective-permute-done((f32[1,2,128,256]{3,2,1,0:T(8,128)S(1)}, f32[1,2,128,256]{3,2,1,0:T(8,128)S(1)}, u32[]{:S(2)}, u32[]{:S(2)}) %collective-permute-start.16) | collective-permute-done | bytes 262176 | tf_op jit(solution)/shard_map/ppermute | solution.py:10
  305.7 5.5 collective-permute-done.17
  313.2 4.1 collective-permute-start.19
  322.4 4.7 collective-permute-done.19
  339.8 10.9 %collective-permute-done.20 = f32[2,2,128,256]{3,2,0,1:T(8,128)S(1)} collective-permute-done((f32[2,2,128,256]{3,2,0,1:T(8,128)S(1)}, f32[2,2,128,256]{3,2,0,1:T(8,128)S(1)}, u32[]{:S(2)}, u32[]{:S(2)}) %collective-permute-start.20) | collective-permute-done | bytes 524320 | tf_op jit(solution)/shard_map/ppermute | solution.py:10
  350.7 9.4 %collective-permute-done.21 = f32[2,2,128,256]{3,2,0,1:T(8,128)S(1)} collective-permute-done((f32[2,2,128,256]{3,2,0,1:T(8,128)S(1)}, f32[2,2,128,256]{3,2,0,1:T(8,128)S(1)}, u32[]{:S(2)}, u32[]{:S(2)}) %collective-permute-start.21) | collective-permute-done | bytes 524320 | tf_op jit(solution)/shard_map/ppermute | solution.py:10
  362.2 4.8 collective-permute-start.23
  367.2 31.1 %collective-permute-done.22 = f32[2,2,128,256]{3,2,0,1:T(8,128)} collective-permute-done((f32[2,2,128,256]{3,2,0,1:T(8,128)S(1)}, f32[2,2,128,256]{3,2,0,1:T(8,128)}, u32[]{:S(2)}, u32[]{:S(2)}) %collective-permute-start.22) | collective-permute-done | bytes 524320 | tf_op jit(solution)/shard_map/ppermute | solution.py:10
  398.3 10.7 %collective-permute-done.23 = f32[2,2,128,256]{3,2,0,1:T(8,128)} collective-permute-done((f32[2,2,128,256]{3,2,0,1:T(8,128)S(1)}, f32[2,2,128,256]{3,2,0,1:T(8,128)}, u32[]{:S(2)}, u32[]{:S(2)}) %collective-permute-start.23) | collective-permute-done | bytes 524320 | tf_op jit(solution)/shard_map/ppermute | solution.py:10
  412.8 7.8 %collective-permute-start.25 = (f32[2,2,128,256]{3,2,0,1:T(8,128)S(1)}, f32[2,2,128,256]{3,2,0,1:T(8,128)}, u32[]{:S(2)}, u32[]{:S(2)}) collective-permute-start(f32[2,2,128,256]{3,2,0,1:T(8,128)S(1)} %get-tuple-element.9), channel_id=1, source_target_pairs={{0,64},{16,80},{32,96},{48,112},{64,0},{80,16},{96,32},{112,48},{1... | collective-permute-start | bytes 1572872 | tf_op jit(solution)/shard_map/ppermute | solution.py:10
  420.8 73.9 %collective-permute-done.24 = f32[2,2,128,256]{3,2,0,1:T(8,128)} collective-permute-done((f32[2,2,128,256]{3,2,0,1:T(8,128)S(1)}, f32[2,2,128,256]{3,2,0,1:T(8,128)}, u32[]{:S(2)}, u32[]{:S(2)}) %collective-permute-start.24) | collective-permute-done | bytes 524320 | tf_op jit(solution)/shard_map/ppermute | solution.py:10
  494.7 11.1 %collective-permute-done.25 = f32[2,2,128,256]{3,2,0,1:T(8,128)} collective-permute-done((f32[2,2,128,256]{3,2,0,1:T(8,128)S(1)}, f32[2,2,128,256]{3,2,0,1:T(8,128)}, u32[]{:S(2)}, u32[]{:S(2)}) %collective-permute-start.25) | collective-permute-done | bytes 524320 | tf_op jit(solution)/shard_map/ppermute | solution.py:10
  513.7 10.8 %collective-permute-done.26 = f32[2,2,128,256]{3,2,0,1:T(8,128)} collective-permute-done((f32[2,2,128,256]{3,2,0,1:T(8,128)S(1)}, f32[2,2,128,256]{3,2,0,1:T(8,128)}, u32[]{:S(2)}, u32[]{:S(2)}) %collective-permute-start.26) | collective-permute-done | bytes 524320 | tf_op jit(solution)/shard_map/ppermute | solution.py:10
  524.5 10.3 %collective-permute-done.27 = f32[2,2,128,256]{3,2,0,1:T(8,128)} collective-permute-done((f32[2,2,128,256]{3,2,0,1:T(8,128)S(1)}, f32[2,2,128,256]{3,2,0,1:T(8,128)}, u32[]{:S(2)}, u32[]{:S(2)}) %collective-permute-start.27) | collective-permute-done | bytes 524320 | tf_op jit(solution)/shard_map/ppermute | solution.py:10
  540.5 13.1 %collective-permute-done.29 = f32[2,2,128,256]{3,2,0,1:T(8,128)} collective-permute-done((f32[2,2,128,256]{3,2,0,1:T(8,128)}, f32[2,2,128,256]{3,2,0,1:T(8,128)}, u32[]{:S(2)}, u32[]{:S(2)}) %collective-permute-start.29) | collective-permute-done | bytes 524320 | tf_op jit(solution)/shard_map/ppermute | solution.py:10
  558.9 12.0 %collective-permute-done.28 = f32[2,2,128,256]{3,2,0,1:T(8,128)S(1)} collective-permute-done((f32[2,2,128,256]{3,2,0,1:T(8,128)S(1)}, f32[2,2,128,256]{3,2,0,1:T(8,128)S(1)}, u32[]{:S(2)}, u32[]{:S(2)}) %collective-permute-start.28) | collective-permute-done | bytes 524320 | tf_op jit(solution)/shard_map/ppermute | solution.py:10
  (105 shorter events, 107.3 us)
Async XLA Ops:
  7.2 176.1 %copy-start = (bf16[4096,256]{1,0:T(8,128)(2,1)S(1)}, bf16[4096,256]{1,0:T(8,128)(2,1)}, u32[]{:S(2)}) copy-start(bf16[4096,256]{1,0:T(8,128)(2,1)} %param.9) | copy-start | bytes 6291460
  7.2 176.1 %all-gather.2.cloned.1.call-start = ((), (), s32[]{:S(2)}) async-start(), calls=%async_computation | async-start | bytes 1114112 | tf_op jit(solution)/shard_map/all_gather | solution.py:121
  8.6 18.3 %collective-permute-start = (f32[2,2,128,256]{3,2,1,0:T(8,128)S(1)}, f32[2,2,128,256]{3,2,1,0:T(8,128)}, u32[]{:S(2)}, u32[]{:S(2)}) collective-permute-start(f32[2,2,128,256]{3,2,1,0:T(8,128)S(1)} %pad_maximum_fusion), channel_id=1, source_target_pairs={{0,256},{16,272},{32,288},{48,304},{64,320},{80,336},{96,352},{112... | collective-permute-start | bytes 1572872 | tf_op jit(solution)/shard_map/ppermute | solution.py:10
  12.8 24.2 %collective-permute-start.1 = (f32[2,2,128,256]{3,2,1,0:T(8,128)}, f32[2,2,128,256]{3,2,1,0:T(8,128)}, u32[]{:S(2)}, u32[]{:S(2)}) collective-permute-start(f32[2,2,128,256]{3,2,1,0:T(8,128)} %stack.57), channel_id=1, source_target_pairs={{0,256},{16,272},{32,288},{48,304},{64,320},{80,336},{96,352},{112... | collective-permute-start | bytes 1572872 | tf_op jit(solution)/shard_map/ppermute | solution.py:10
  39.2 16.7 %collective-permute-start.2 = (f32[2,2,128,256]{3,2,1,0:T(8,128)S(1)}, f32[2,2,128,256]{3,2,1,0:T(8,128)S(1)}, u32[]{:S(2)}, u32[]{:S(2)}) collective-permute-start(f32[2,2,128,256]{3,2,1,0:T(8,128)S(1)} %get-tuple-element.20), channel_id=1, source_target_pairs={{0,128},{16,144},{32,160},{48,176},{64,192},{80,208},{96,224},{112... | collective-permute-start | bytes 1572872 | tf_op jit(solution)/shard_map/ppermute | solution.py:10
  41.9 23.3 %collective-permute-start.3 = (f32[2,2,128,256]{3,2,1,0:T(8,128)}, f32[2,2,128,256]{3,2,1,0:T(8,128)}, u32[]{:S(2)}, u32[]{:S(2)}) collective-permute-start(f32[2,2,128,256]{3,2,1,0:T(8,128)} %get-tuple-element.21), channel_id=1, source_target_pairs={{0,128},{16,144},{32,160},{48,176},{64,192},{80,208},{96,224},{112... | collective-permute-start | bytes 1572872 | tf_op jit(solution)/shard_map/ppermute | solution.py:10
  67.1 96.5 %collective-permute-start.4 = (f32[2,2,128,256]{3,2,1,0:T(8,128)S(1)}, f32[2,2,128,256]{3,2,1,0:T(8,128)}, u32[]{:S(2)}, u32[]{:S(2)}) collective-permute-start(f32[2,2,128,256]{3,2,1,0:T(8,128)S(1)} %get-tuple-element.18), channel_id=1, source_target_pairs={{0,64},{16,80},{32,96},{48,112},{64,0},{80,16},{96,32},{112,48},{1... | collective-permute-start | bytes 1572872 | tf_op jit(solution)/shard_map/ppermute | solution.py:10
  76.1 98.6 %collective-permute-start.5 = (f32[2,2,128,256]{3,2,1,0:T(8,128)S(1)}, f32[2,2,128,256]{3,2,1,0:T(8,128)}, u32[]{:S(2)}, u32[]{:S(2)}) collective-permute-start(f32[2,2,128,256]{3,2,1,0:T(8,128)S(1)} %get-tuple-element.19), channel_id=1, source_target_pairs={{0,64},{16,80},{32,96},{48,112},{64,0},{80,16},{96,32},{112,48},{1... | collective-permute-start | bytes 1572872 | tf_op jit(solution)/shard_map/ppermute | solution.py:10
  176.5 35.6 %collective-permute-start.6 = (f32[2,2,128,256]{3,2,1,0:T(8,128)S(1)}, f32[2,2,128,256]{3,2,1,0:T(8,128)}, u32[]{:S(2)}, u32[]{:S(2)}) collective-permute-start(f32[2,2,128,256]{3,2,1,0:T(8,128)S(1)} %get-tuple-element.16), channel_id=1, source_target_pairs={{0,32},{16,48},{32,0},{48,16},{64,96},{80,112},{96,64},{112,80},{1... | collective-permute-start | bytes 1572872 | tf_op jit(solution)/shard_map/ppermute | solution.py:10
  178.4 41.9 %collective-permute-start.7 = (f32[2,2,128,256]{3,2,1,0:T(8,128)S(1)}, f32[2,2,128,256]{3,2,1,0:T(8,128)}, u32[]{:S(2)}, u32[]{:S(2)}) collective-permute-start(f32[2,2,128,256]{3,2,1,0:T(8,128)S(1)} %get-tuple-element.17), channel_id=1, source_target_pairs={{0,32},{16,48},{32,0},{48,16},{64,96},{80,112},{96,64},{112,80},{1... | collective-permute-start | bytes 1572872 | tf_op jit(solution)/shard_map/ppermute | solution.py:10
  187.3 12.9 %collective-permute-start.10 = (f32[1,2,128,256]{3,2,1,0:T(8,128)}, f32[1,2,128,256]{3,2,1,0:T(8,128)}, u32[]{:S(2)}, u32[]{:S(2)}) collective-permute-start(f32[1,2,128,256]{3,2,1,0:T(8,128)} %pad_maximum_fusion.4), channel_id=1, source_target_pairs={{0,256},{16,272},{32,288},{48,304},{64,320},{80,336},{96,352},{112... | collective-permute-start | bytes 786440 | tf_op jit(solution)/shard_map/ppermute | solution.py:10
  191.4 12.9 %collective-permute-start.11 = (f32[1,2,128,256]{3,2,1,0:T(8,128)}, f32[1,2,128,256]{3,2,1,0:T(8,128)}, u32[]{:S(2)}, u32[]{:S(2)}) collective-permute-start(f32[1,2,128,256]{3,2,1,0:T(8,128)} %stack.61), channel_id=1, source_target_pairs={{0,256},{16,272},{32,288},{48,304},{64,320},{80,336},{96,352},{112... | collective-permute-start | bytes 786440 | tf_op jit(solution)/shard_map/ppermute | solution.py:10
  206.2 22.5 %collective-permute-start.12 = (f32[1,2,128,256]{3,2,1,0:T(8,128)}, f32[1,2,128,256]{3,2,1,0:T(8,128)}, u32[]{:S(2)}, u32[]{:S(2)}) collective-permute-start(f32[1,2,128,256]{3,2,1,0:T(8,128)} %get-tuple-element.38), channel_id=1, source_target_pairs={{0,128},{16,144},{32,160},{48,176},{64,192},{80,208},{96,224},{112... | collective-permute-start | bytes 786440 | tf_op jit(solution)/shard_map/ppermute | solution.py:10
  209.0 19.8 %collective-permute-start.13 = (f32[1,2,128,256]{3,2,1,0:T(8,128)}, f32[1,2,128,256]{3,2,1,0:T(8,128)}, u32[]{:S(2)}, u32[]{:S(2)}) collective-permute-start(f32[1,2,128,256]{3,2,1,0:T(8,128)} %get-tuple-element.39), channel_id=1, source_target_pairs={{0,128},{16,144},{32,160},{48,176},{64,192},{80,208},{96,224},{112... | collective-permute-start | bytes 786440 | tf_op jit(solution)/shard_map/ppermute | solution.py:10
  222.8 17.2 %collective-permute-start.8 = (f32[2,2,128,256]{3,2,1,0:T(8,128)}, f32[2,2,128,256]{3,2,1,0:T(8,128)S(1)}, u32[]{:S(2)}, u32[]{:S(2)}) collective-permute-start(f32[2,2,128,256]{3,2,1,0:T(8,128)} %get-tuple-element.14), channel_id=1, source_target_pairs={{0,16},{16,0},{32,48},{48,32},{64,80},{80,64},{96,112},{112,96},{1... | collective-permute-start | bytes 1572872 | tf_op jit(solution)/shard_map/ppermute | solution.py:10
  224.7 31.1 %collective-permute-start.9 = (f32[2,2,128,256]{3,2,1,0:T(8,128)}, f32[2,2,128,256]{3,2,1,0:T(8,128)S(1)}, u32[]{:S(2)}, u32[]{:S(2)}) collective-permute-start(f32[2,2,128,256]{3,2,1,0:T(8,128)} %get-tuple-element.15), channel_id=1, source_target_pairs={{0,16},{16,0},{32,48},{48,32},{64,80},{80,64},{96,112},{112,96},{1... | collective-permute-start | bytes 1572872 | tf_op jit(solution)/shard_map/ppermute | solution.py:10
  230.1 29.5 %collective-permute-start.14 = (f32[1,2,128,256]{3,2,1,0:T(8,128)S(1)}, f32[1,2,128,256]{3,2,1,0:T(8,128)S(1)}, u32[]{:S(2)}, u32[]{:S(2)}) collective-permute-start(f32[1,2,128,256]{3,2,1,0:T(8,128)S(1)} %get-tuple-element.36), channel_id=1, source_target_pairs={{0,64},{16,80},{32,96},{48,112},{64,0},{80,16},{96,32},{112,48},{1... | collective-permute-start | bytes 786440 | tf_op jit(solution)/shard_map/ppermute | solution.py:10
  238.1 33.7 %collective-permute-start.15 = (f32[1,2,128,256]{3,2,1,0:T(8,128)S(1)}, f32[1,2,128,256]{3,2,1,0:T(8,128)S(1)}, u32[]{:S(2)}, u32[]{:S(2)}) collective-permute-start(f32[1,2,128,256]{3,2,1,0:T(8,128)S(1)} %get-tuple-element.37), channel_id=1, source_target_pairs={{0,64},{16,80},{32,96},{48,112},{64,0},{80,16},{96,32},{112,48},{1... | collective-permute-start | bytes 786440 | tf_op jit(solution)/shard_map/ppermute | solution.py:10
  271.9 33.8 %collective-permute-start.16 = (f32[1,2,128,256]{3,2,1,0:T(8,128)S(1)}, f32[1,2,128,256]{3,2,1,0:T(8,128)S(1)}, u32[]{:S(2)}, u32[]{:S(2)}) collective-permute-start(f32[1,2,128,256]{3,2,1,0:T(8,128)S(1)} %get-tuple-element.34), channel_id=1, source_target_pairs={{0,32},{16,48},{32,0},{48,16},{64,96},{80,112},{96,64},{112,80},{1... | collective-permute-start | bytes 786440 | tf_op jit(solution)/shard_map/ppermute | solution.py:10
  285.6 25.6 %collective-permute-start.17 = (f32[1,2,128,256]{3,2,1,0:T(8,128)S(1)}, f32[1,2,128,256]{3,2,1,0:T(8,128)S(1)}, u32[]{:S(2)}, u32[]{:S(2)}) collective-permute-start(f32[1,2,128,256]{3,2,1,0:T(8,128)S(1)} %get-tuple-element.35), channel_id=1, source_target_pairs={{0,32},{16,48},{32,0},{48,16},{64,96},{80,112},{96,64},{112,80},{1... | collective-permute-start | bytes 786440 | tf_op jit(solution)/shard_map/ppermute | solution.py:10
  311.3 11.1 %collective-permute-start.18 = (f32[1,2,128,256]{3,2,1,0:T(8,128)S(1)}, f32[1,2,128,256]{3,2,1,0:T(8,128)S(1)}, u32[]{:S(2)}, u32[]{:S(2)}) collective-permute-start(f32[1,2,128,256]{3,2,1,0:T(8,128)S(1)} %get-tuple-element.32), channel_id=1, source_target_pairs={{0,16},{16,0},{32,48},{48,32},{64,80},{80,64},{96,112},{112,96},{1... | collective-permute-start | bytes 786440 | tf_op jit(solution)/shard_map/ppermute | solution.py:10
  313.2 13.8 %collective-permute-start.19 = (f32[1,2,128,256]{3,2,1,0:T(8,128)S(1)}, f32[1,2,128,256]{3,2,1,0:T(8,128)S(1)}, u32[]{:S(2)}, u32[]{:S(2)}) collective-permute-start(f32[1,2,128,256]{3,2,1,0:T(8,128)S(1)} %get-tuple-element.33), channel_id=1, source_target_pairs={{0,16},{16,0},{32,48},{48,32},{64,80},{80,64},{96,112},{112,96},{1... | collective-permute-start | bytes 786440 | tf_op jit(solution)/shard_map/ppermute | solution.py:10
  333.9 16.8 %collective-permute-start.20 = (f32[2,2,128,256]{3,2,0,1:T(8,128)S(1)}, f32[2,2,128,256]{3,2,0,1:T(8,128)S(1)}, u32[]{:S(2)}, u32[]{:S(2)}) collective-permute-start(f32[2,2,128,256]{3,2,0,1:T(8,128)S(1)} %get-tuple-element.28), channel_id=1, source_target_pairs={{0,16},{16,0},{32,48},{48,32},{64,80},{80,64},{96,112},{112,96},{1... | collective-permute-start | bytes 1572872 | tf_op jit(solution)/shard_map/ppermute | solution.py:10
  336.1 23.9 %collective-permute-start.21 = (f32[2,2,128,256]{3,2,0,1:T(8,128)S(1)}, f32[2,2,128,256]{3,2,0,1:T(8,128)S(1)}, u32[]{:S(2)}, u32[]{:S(2)}) collective-permute-start(f32[2,2,128,256]{3,2,0,1:T(8,128)S(1)} %get-tuple-element.29), channel_id=1, source_target_pairs={{0,16},{16,0},{32,48},{48,32},{64,80},{80,64},{96,112},{112,96},{1... | collective-permute-start | bytes 1572872 | tf_op jit(solution)/shard_map/ppermute | solution.py:10
  360.3 38.0 %collective-permute-start.22 = (f32[2,2,128,256]{3,2,0,1:T(8,128)S(1)}, f32[2,2,128,256]{3,2,0,1:T(8,128)}, u32[]{:S(2)}, u32[]{:S(2)}) collective-permute-start(f32[2,2,128,256]{3,2,0,1:T(8,128)S(1)} %get-tuple-element.10), channel_id=1, source_target_pairs={{0,32},{16,48},{32,0},{48,16},{64,96},{80,112},{96,64},{112,80},{1... | collective-permute-start | bytes 1572872 | tf_op jit(solution)/shard_map/ppermute | solution.py:10
  362.2 46.8 %collective-permute-start.23 = (f32[2,2,128,256]{3,2,0,1:T(8,128)S(1)}, f32[2,2,128,256]{3,2,0,1:T(8,128)}, u32[]{:S(2)}, u32[]{:S(2)}) collective-permute-start(f32[2,2,128,256]{3,2,0,1:T(8,128)S(1)} %get-tuple-element.11), channel_id=1, source_target_pairs={{0,32},{16,48},{32,0},{48,16},{64,96},{80,112},{96,64},{112,80},{1... | collective-permute-start | bytes 1572872 | tf_op jit(solution)/shard_map/ppermute | solution.py:10
  410.9 83.8 %collective-permute-start.24 = (f32[2,2,128,256]{3,2,0,1:T(8,128)S(1)}, f32[2,2,128,256]{3,2,0,1:T(8,128)}, u32[]{:S(2)}, u32[]{:S(2)}) collective-permute-start(f32[2,2,128,256]{3,2,0,1:T(8,128)S(1)} %get-tuple-element.8), channel_id=1, source_target_pairs={{0,64},{16,80},{32,96},{48,112},{64,0},{80,16},{96,32},{112,48},{1... | collective-permute-start | bytes 1572872 | tf_op jit(solution)/shard_map/ppermute | solution.py:10
  412.8 93.1 %collective-permute-start.25 = (f32[2,2,128,256]{3,2,0,1:T(8,128)S(1)}, f32[2,2,128,256]{3,2,0,1:T(8,128)}, u32[]{:S(2)}, u32[]{:S(2)}) collective-permute-start(f32[2,2,128,256]{3,2,0,1:T(8,128)S(1)} %get-tuple-element.9), channel_id=1, source_target_pairs={{0,64},{16,80},{32,96},{48,112},{64,0},{80,16},{96,32},{112,48},{1... | collective-permute-start | bytes 1572872 | tf_op jit(solution)/shard_map/ppermute | solution.py:10
  507.7 16.8 %collective-permute-start.26 = (f32[2,2,128,256]{3,2,0,1:T(8,128)S(1)}, f32[2,2,128,256]{3,2,0,1:T(8,128)}, u32[]{:S(2)}, u32[]{:S(2)}) collective-permute-start(f32[2,2,128,256]{3,2,0,1:T(8,128)S(1)} %get-tuple-element.6), channel_id=1, source_target_pairs={{0,128},{16,144},{32,160},{48,176},{64,192},{80,208},{96,224},{112... | collective-permute-start | bytes 1572872 | tf_op jit(solution)/shard_map/ppermute | solution.py:10
  510.4 24.3 %collective-permute-start.27 = (f32[2,2,128,256]{3,2,0,1:T(8,128)S(1)}, f32[2,2,128,256]{3,2,0,1:T(8,128)}, u32[]{:S(2)}, u32[]{:S(2)}) collective-permute-start(f32[2,2,128,256]{3,2,0,1:T(8,128)S(1)} %get-tuple-element.7), channel_id=1, source_target_pairs={{0,128},{16,144},{32,160},{48,176},{64,192},{80,208},{96,224},{112... | collective-permute-start | bytes 1572872 | tf_op jit(solution)/shard_map/ppermute | solution.py:10
  536.9 16.7 %collective-permute-start.29 = (f32[2,2,128,256]{3,2,0,1:T(8,128)}, f32[2,2,128,256]{3,2,0,1:T(8,128)}, u32[]{:S(2)}, u32[]{:S(2)}) collective-permute-start(f32[2,2,128,256]{3,2,0,1:T(8,128)} %add_select_fusion.1), channel_id=1, source_target_pairs={{0,256},{16,272},{32,288},{48,304},{64,320},{80,336},{96,352},{112... | collective-permute-start | bytes 1572872 | tf_op jit(solution)/shard_map/ppermute | solution.py:10
  555.4 15.5 %collective-permute-start.28 = (f32[2,2,128,256]{3,2,0,1:T(8,128)S(1)}, f32[2,2,128,256]{3,2,0,1:T(8,128)S(1)}, u32[]{:S(2)}, u32[]{:S(2)}) collective-permute-start(f32[2,2,128,256]{3,2,0,1:T(8,128)S(1)} %get-tuple-element.5), channel_id=1, source_target_pairs={{0,256},{16,272},{32,288},{48,304},{64,320},{80,336},{96,352},{112... | collective-permute-start | bytes 1572872 | tf_op jit(solution)/shard_map/ppermute | solution.py:10
  (14 other events, 526.3 us)
Sparse Core Ops, SparseCore 0:
  16.9 82.1 all-gather.1
where the time goes:
time: 582 us; the launch traced here: 581 us
  waiting for transfers between devices  405 us (70%)
  starting transfers between devices  116 us (20%)
  other arithmetic  27 us (5%)
  between operations  16 us (3%)
  matrix products  13.2 us (2%)
    ppermute x30, waiting for transfers between devices, from_partner(): lax.ppermute(x, axis, [(i, i ^ 1 << apart) for i in range(lax.axis_size(a...  405 us
    ppermute x30, starting transfers between devices, from_partner(): lax.ppermute(x, axis, [(i, i ^ 1 << apart) for i in range(lax.axis_size(a...  116 us
    select_n x10, other arithmetic, forward_transform(): real_part = jnp.where(upper_side, diff_real, real_part + other_real)  13.2 us
  transfers between devices with their start and end apart: 31, of which 25 were waited for; matrix products, arithmetic and copies ran while one was open for 4% of the time, Pallas kernels for 0%

commit v1 on v0

v1 whole, which is shorter than its diff:
```python
import functools
import math

import jax
import jax.numpy as jnp
import numpy as np
from jax import lax
from jax.experimental import pallas as pl
from jax.experimental.pallas import tpu as pltpu
from jax.sharding import Mesh
from jax.sharding import PartitionSpec as P

F32 = jnp.float32
BF16 = jnp.bfloat16
CTX = ("x", "zl")
TP = ("zh", "y", "core")
VMEM = pl.BlockSpec(memory_space=pltpu.VMEM)
SMEM = pl.BlockSpec(memory_space=pltpu.SMEM)
PARAMS = pltpu.CompilerParams(vmem_limit_bytes=48 * 1024 * 1024)


def split_table(table):
    high = table.astype(np.float32).astype(jnp.bfloat16)
    low = (table - high.astype(np.float64)).astype(np.float32).astype(jnp.bfloat16)
    return high, low


def tables(blocks, lanes, chans):
    total = blocks * lanes
    k1 = np.arange(blocks)
    angle = 2.0 * np.pi * np.outer(k1 + 0.25, np.arange(blocks)) / blocks
    eye = np.eye(chans)
    rows = np.concatenate([np.kron(np.cos(angle), eye), np.kron(-np.sin(angle), eye)], axis=0)
    b = np.arange(lanes)
    turn = 2.0 * np.pi * np.outer(k1 + 0.25, b) / total
    twist_re = np.repeat(np.cos(turn), chans, axis=0).astype(np.float32)
    twist_im = np.repeat(-np.sin(turn), chans, axis=0).astype(np.float32)
    lane_angle = 2.0 * np.pi * np.outer(b, b) / lanes
    c, s = np.cos(lane_angle), np.sin(lane_angle)
    lane = np.block([[c, -s], [s, c]])
    return rows, lane, twist_re, twist_im


def halves(x):
    high = x.astype(BF16)
    return high, (x - high.astype(F32)).astype(BF16)


def dot3(a, b):
    a_high, a_low = a
    b_high, b_low = b
    dot = functools.partial(jnp.dot, preferred_element_type=F32)
    return dot(a_high, b_high) + (dot(a_high, b_low) + dot(a_low, b_high))


def forward(x, rows, lane, twist_re, twist_im):
    n = x.shape[0]
    first = dot3(rows, halves(x))
    re, im = first[:n], first[n:]
    turned = jnp.concatenate([re * twist_re - im * twist_im, re * twist_im + im * twist_re], axis=1)
    return dot3(halves(turned), lane)


def prep_kernel(scale, filter_ref, keys_ref, values_ref, out_ref):
    chans = out_ref.shape[1] // 2
    shape = (out_ref.shape[0], chans, out_ref.shape[2])
    out_ref[:, :chans, :] = (filter_ref[...] * scale).T.reshape(shape)
    gated = keys_ref[...].astype(F32) * values_ref[...].astype(F32)
    out_ref[:, chans:, :] = gated.T.reshape(shape)


def matmul_kernel(place_ref, near_ref, far_ref, proj_ref, queries_ref, conv_ref, grad_q_ref, grad_ref, turned_ref):
    n_y, n_zh, _, width = near_ref.shape
    zh, core = place_ref[0], place_ref[1]
    total = jnp.zeros(grad_ref.shape, F32)
    for ref, which in ((near_ref, 0), (far_ref, 1)):
        for y in range(n_y):
            for other in range(n_zh):
                part = ((zh ^ other) * n_y + y) * 2 + (core ^ which)
                weights = proj_ref[pl.ds(pl.multiple_of(part * width, width), width), :]
                total += jnp.dot(ref[y, other], weights, preferred_element_type=F32)
    grad_q_ref[...] = (total * conv_ref[...].astype(F32)).astype(BF16)
    grad = total * queries_ref[...].astype(F32)
    grad_ref[...] = grad
    turned_ref[...] = grad.T.reshape(turned_ref.shape)


def spectra_kernel(x_ref, rh, rl, lh, ll, tr, ti, out_ref):
    blocks, both, lanes = x_ref.shape
    chans = both // 2
    for field in range(2):
        x = x_ref[:, field * chans : (field + 1) * chans, :].reshape(blocks * chans, lanes)
        out_ref[field] = forward(x, (rh[...], rl[...]), (lh[...], ll[...]), tr[...], ti[...])


def correlate_kernel(scale, x_ref, spec_ref, rh, rl, lh, ll, rth, rtl, lth, ltl, tr, ti, out_ref):
    blocks, chans, lanes = x_ref.shape
    n = blocks * chans
    twist_re, twist_im = tr[...], ti[...]
    grad = forward(x_ref[...].reshape(n, lanes), (rh[...], rl[...]), (lh[...], ll[...]), twist_re, twist_im)
    g_re, g_im = grad[:, :lanes] * scale, grad[:, lanes:] * scale
    sides = []
    for field in range(2):
        s_re, s_im = spec_ref[field, :, :lanes], spec_ref[field, :, lanes:]
        prod = jnp.concatenate([s_re * g_re + s_im * g_im, s_re * g_im - s_im * g_re], axis=1)
        back = dot3(halves(prod), (lth[...], ltl[...]))
        re, im = back[:, :lanes], back[:, lanes:]
        sides.append(jnp.concatenate([re * twist_re + im * twist_im, im * twist_re - re * twist_im], axis=0))
    result = dot3((rth[...], rtl[...]), halves(jnp.concatenate(sides, axis=1)))
    for field in range(2):
        out_ref[:, field * chans : (field + 1) * chans, :] = result[:, field * lanes : (field + 1) * lanes].reshape(
            blocks, chans, lanes
        )


def final_kernel(scale, x_ref, grad_ref, keys_ref, values_ref, skip_ref, grad_k_ref, grad_v_ref, filter_grad_ref):
    blocks, both, lanes = x_ref.shape
    chans = both // 2
    conv = x_ref[:, :chans, :].reshape(blocks * chans, lanes).T
    input_grad = conv + skip_ref[...] * grad_ref[...]
    grad_k_ref[...] = (input_grad * values_ref[...].astype(F32)).astype(BF16)
    grad_v_ref[...] = (input_grad * keys_ref[...].astype(F32)).astype(BF16)
    filter_grad_ref[...] = x_ref[:, chans:, :].reshape(blocks * chans, lanes).T * scale


def call(kernel, outs, n_in, scalars=0):
    return pl.pallas_call(
        kernel,
        out_shape=outs,
        in_specs=[SMEM] * scalars + [VMEM] * (n_in - scalars),
        out_specs=jax.tree.map(lambda _: VMEM, outs),
        compiler_params=PARAMS,
    )


def body(out_grad, out_proj, queries, keys, values, conv_out, long_filter, skip_gain):
    tok, width = queries.shape
    n_ctx = lax.axis_size("x") * lax.axis_size("zl")
    chans = width // n_ctx
    total_len = tok * n_ctx
    inv_root = 1.0 / math.sqrt(total_len)
    shape = jax.ShapeDtypeStruct

    rows, lane, twist_re, twist_im = tables(n_ctx, tok, chans)
    fwd = [jnp.asarray(t) for t in (*split_table(rows), *split_table(lane))]
    inv = [jnp.asarray(t) for t in (*split_table(rows.T), *split_table(lane.T))]
    twist = [jnp.asarray(twist_re), jnp.asarray(twist_im)]

    far = lax.ppermute(out_grad, "zh", [(0, 1), (1, 0)])
    prepared = call(functools.partial(prep_kernel, inv_root), shape((n_ctx, 2 * chans, tok), F32), 3)(
        long_filter, keys, values
    )
    fields = lax.all_to_all(prepared, CTX, 0, 0)

    near = lax.all_gather(jnp.stack([out_grad, far]), "y")
    across = lax.ppermute(near, "core", [(0, 1), (1, 0)])
    place = jnp.stack([lax.axis_index("zh"), lax.axis_index("core")]).astype(jnp.int32)
    grad_q, grad, turned = call(
        matmul_kernel,
        (shape((tok, width), BF16), shape((tok, width), F32), shape((n_ctx, chans, tok), F32)),
        6,
        1,
    )(place, near, across, out_proj, queries, conv_out)
    turned = lax.all_to_all(turned, CTX, 0, 0)

    spec = call(spectra_kernel, shape((2, n_ctx * chans, 2 * tok), F32), 7)(fields, *fwd, *twist)
    corr = call(
        functools.partial(correlate_kernel, 1.0 / total_len), shape((n_ctx, 2 * chans, tok), F32), 12
    )(turned, spec, *fwd, *inv, *twist)
    corr = lax.all_to_all(corr, CTX, 0, 0)
    grad_k, grad_v, filter_grad = call(
        functools.partial(final_kernel, inv_root),
        (shape((tok, width), BF16), shape((tok, width), BF16), shape((tok, width), F32)),
        5,
    )(corr, grad, keys, values, skip_gain[None, :])
    return grad_q, grad_k, grad_v, filter_grad


def solution(mesh):
    fine = Mesh(mesh.devices.reshape(4, 8, 2, 4, 2), CTX + TP)
    return jax.shard_map(
        body,
        mesh=fine,
        in_specs=(P(CTX, TP), P(None, TP), P(CTX, TP), P(CTX, TP), P(CTX, TP), P(CTX, TP), P(CTX, TP), P(TP)),
        out_specs=(P(CTX, TP), P(CTX, TP), P(CTX, TP), P(CTX, TP)),
        check_vma=False,
    )
```

time: 582 us -> 118 us (0.20)
  the two profiles are of different devices: /device:TPU:6 before, /device:TPU:1 now
where the time goes in v1:
time: 118 us; the launch traced here: 117 us
  starting transfers between devices  48.2 us (41%)
  blocking collectives  36.9 us (31%)
  waiting for transfers between devices  17.9 us (15%)
  Pallas kernels  6.46 us (5%)
  local copies, waits for them, and re-layouts  5.91 us (5%)
    all_to_all x1, blocking collectives, body(): corr = lax.all_to_all(corr, CTX, 0, 0)  25.6 us
    all_to_all x1, starting transfers between devices, body(): turned = lax.all_to_all(turned, CTX, 0, 0)  18.3 us
    all_to_all x1, starting transfers between devices, body(): fields = lax.all_to_all(prepared, CTX, 0, 0)  16.1 us
    all_gather x1, blocking collectives, body(): near = lax.all_gather(jnp.stack([out_grad, far]), 'y')  11.3 us
    all_to_all x1, waiting for transfers between devices, body(): turned = lax.all_to_all(turned, CTX, 0, 0)  10.2 us
    ppermute x1, starting transfers between devices, body(): far = lax.ppermute(out_grad, 'zh', [(0, 1), (1, 0)])  7.94 us
    ppermute x1, waiting for transfers between devices, body(): far = lax.ppermute(out_grad, 'zh', [(0, 1), (1, 0)])  6.28 us
    ppermute x1, starting transfers between devices, body(): across = lax.ppermute(near, 'core', [(0, 1), (1, 0)])  5.99 us
  transfers between devices with their start and end apart: 4, of which 3 were waited for; matrix products, arithmetic and copies ran while one was open for 1% of the time, Pallas kernels for 3%

profile of v1, /device:TPU:1, one launch (start us, length us, event | category | flops | bytes accessed | tf_op | source)
XLA Modules:
  0.0 117.3 jit_solution(16080995391244418803)
XLA Ops:
  0.6 0.0 copy-start.9
  0.6 0.8 copy-done.9
  1.5 0.8 copy-done.11
  2.3 0.9 copy-done.13
  3.2 0.8 shard_map.202
  4.1 16.1 %all-to-all-start.1 = ((f32[32,16,128]{2,1,0:T(8,128)}), f32[32,16,128]{2,1,0:T(8,128)S(1)}, u32[]{:S(2)}, u32[]{:S(2)}) async-start(f32[32,16,128]{2,1,0:T(8,128)} %shard_map.202), calls=%async_computation.1 | async-start | bytes 524288 | tf_op jit(solution)/shard_map/all_to_all | solution.py:153
  20.1 7.9 %collective-permute-start = (bf16[128,256]{1,0:T(8,128)(2,1)}, bf16[128,256]{1,0:T(8,128)(2,1)S(1)}, u32[]{:S(2)}, u32[]{:S(2)}) collective-permute-start(bf16[128,256]{1,0:T(8,128)(2,1)} %param.18), channel_id=1, source_target_pairs={{0,8},{8,0},{1,9},{9,1},{2,10},{10,2},{3,11},{11,3},{4,12},{12,4},... | collective-permute-start | bytes 196616 | tf_op jit(solution)/shard_map/ppermute | solution.py:149
  28.1 6.3 %collective-permute-done = bf16[128,256]{1,0:T(8,128)(2,1)S(1)} collective-permute-done((bf16[128,256]{1,0:T(8,128)(2,1)}, bf16[128,256]{1,0:T(8,128)(2,1)S(1)}, u32[]{:S(2)}, u32[]{:S(2)}) %collective-permute-start) | collective-permute-done | bytes 65568 | tf_op jit(solution)/shard_map/ppermute | solution.py:149
  34.4 0.9 pad_maximum_fusion
  35.3 0.0 copy-start.1
  35.3 0.0 copy-start.2
  35.3 0.0 copy-start.3
  35.3 11.3 %all-gather = bf16[8,128,256]{2,1,0:T(8,128)(2,1)S(1)} all-gather(bf16[2,128,256]{2,1,0:T(8,128)(2,1)S(1)} %pad_maximum_fusion), channel_id=2, replica_groups=mesh['x'=4,'zl'=8,'zh'=2,'y'=4,'core'=2] {'y'}, dimensions={0}, use_global_device_ids=true | all-gather | bytes 655360 | tf_op jit(solution)/shard_map/all_gather | solution.py:155
  46.6 6.0 %collective-permute-start.1 = (bf16[4,2,128,256]{3,2,1,0:T(8,128)(2,1)S(1)}, bf16[4,2,128,256]{3,2,1,0:T(8,128)(2,1)S(1)}, u32[]{:S(2)}, u32[]{:S(2)}) collective-permute-start(bf16[4,2,128,256]{3,2,1,0:T(8,128)(2,1)S(1)} %bitcast.6), channel_id=1, source_target_pairs={{0,1},{1,0},{2,3},{3,2},{4,5},{5,4},{6,7},{7,6},{8,9},{9,8},{10,11... | collective-permute-start | bytes 1572872 | tf_op jit(solution)/shard_map/ppermute | solution.py:156
  52.6 0.1 pad_add_fusion.place_ref
  52.7 1.4 %collective-permute-done.1.far_ref = bf16[4,2,128,256]{3,2,1,0:T(8,128)(2,1)S(1)} collective-permute-done((bf16[4,2,128,256]{3,2,1,0:T(8,128)(2,1)S(1)}, bf16[4,2,128,256]{3,2,1,0:T(8,128)(2,1)S(1)}, u32[]{:S(2)}, u32[]{:S(2)}) %collective-permute-start.1) | collective-permute-done | bytes 524320 | tf_op jit(solution)/shard_map/ppermute | solution.py:156
  54.2 1.6 %copy-done = bf16[4096,256]{1,0:T(8,128)(2,1)S(1)} copy-done((bf16[4096,256]{1,0:T(8,128)(2,1)S(1)}, bf16[4096,256]{1,0:T(8,128)(2,1)}, u32[]{:S(2)}) %copy-start) | copy-done | bytes 2097176
  55.7 0.8 copy-done.16
  56.6 0.8 copy-done.17
  57.4 1.7 %shard_map.201 = (bf16[128,256]{1,0:T(8,128)(2,1)}, f32[128,256]{1,0:T(8,128)S(1)}, f32[32,8,128]{2,1,0:T(8,128)}) custom-call(s32[2]{0:T(128)S(1)} %pad_add_fusion.place_ref, bf16[4,2,128,256]{3,2,1,0:T(8,128)(2,1)S(1)} %bitcast.7, bf16[4,2,128,256]{3,2,1,0:T(8,128)(2,1)S(1)} %collective-permute-done.1.far_ref, bf16[4096,256]{1,0:T(8,128)(2,1)S(1)} %copy-done, ...), custom_call_target="tpu_custom_call" | custom-call | tf_op jit(solution)/shard_map/pallas_call | solution.py:158
  59.2 0.0 all-to-all-done.1.x_ref
  59.2 18.3 %all-to-all-start = ((f32[32,8,128]{2,1,0:T(8,128)}), f32[32,8,128]{2,1,0:T(8,128)S(1)}, u32[]{:S(2)}, u32[]{:S(2)}) async-start(f32[32,8,128]{2,1,0:T(8,128)} %get-tuple-element.11), calls=%async_computation | async-start | bytes 262144 | tf_op jit(solution)/shard_map/all_to_all | solution.py:164
  77.5 1.5 %shard_map.203.spec_ref = f32[2,256,256]{2,1,0:T(8,128)S(1)} custom-call(f32[32,16,128]{2,1,0:T(8,128)S(1)} %all-to-all-done.1.x_ref, bf16[512,256]{1,0:T(8,128)(2,1)S(1)} %copy-done.1, bf16[512,256]{1,0:T(8,128)(2,1)S(1)} %copy-done.2, bf16[256,256]{1,0:T(8,128)(2,1)S(1)} %copy-done.3, bf16[256,256]{1,0:T(8,128)(2,1)S(1)} %copy-done.4, ...), custom_call_target="tpu_custom_call" | custom-call | tf_op jit(solution)/shard_map/pallas_call | solution.py:166
  79.0 0.0 copy-start.10
  79.0 0.0 copy-start.12
  79.0 0.0 copy-start.18
  79.0 10.2 %all-to-all-done.x_ref = f32[32,8,128]{2,1,0:T(8,128)S(1)} async-done(((f32[32,8,128]{2,1,0:T(8,128)}), f32[32,8,128]{2,1,0:T(8,128)S(1)}, u32[]{:S(2)}, u32[]{:S(2)}) %all-to-all-start) | async-done | bytes 131104 | tf_op jit(solution)/shard_map/all_to_all | solution.py:164
  89.2 0.0 copy-done.7
  89.2 0.0 copy-done.14
  89.2 1.6 %shard_map.204 = f32[32,16,128]{2,1,0:T(8,128)S(1)} custom-call(f32[32,8,128]{2,1,0:T(8,128)S(1)} %all-to-all-done.x_ref, f32[2,256,256]{2,1,0:T(8,128)S(1)} %shard_map.203.spec_ref, bf16[512,256]{1,0:T(8,128)(2,1)S(1)} %copy-done.1, bf16[512,256]{1,0:T(8,128)(2,1)S(1)} %copy-done.2, bf16[256,256]{1,0:T(8,128)(2,1)S(1)} %copy-done.3, ...), custom_call_target="tpu_custom_call" | custom-call | tf_op jit(solution)/shard_map/pallas_call | solution.py:167
  90.9 25.6 %all_to_all.15.x_ref = f32[32,16,128]{2,1,0:T(8,128)S(1)} all-to-all(f32[32,16,128]{2,1,0:T(8,128)S(1)} %shard_map.204), channel_id=1, replica_groups=mesh['x'=4,'zl'=8,'zh'=2,'y'=4,'core'=2] {'x','zl'}, dimensions={0} | all-to-all | bytes 524288 | tf_op jit(solution)/shard_map/all_to_all | solution.py:170
  116.5 0.8 shard_map.205
  (23 shorter events, 0.0 us)
Async XLA Ops:
  0.6 0.8 copy-start.9
  1.5 0.8 copy-start.11
  2.3 0.9 copy-start.13
  4.1 73.4 %copy-start.6 = (f32[256,128]{1,0:T(8,128)S(1)}, f32[256,128]{1,0:T(8,128)}, u32[]{:S(2)}) copy-start(f32[256,128]{1,0:T(8,128)} %constant.37.clone.ti) | copy-start | bytes 393220
  4.1 55.1 %all-to-all-start.1 = ((f32[32,16,128]{2,1,0:T(8,128)}), f32[32,16,128]{2,1,0:T(8,128)S(1)}, u32[]{:S(2)}, u32[]{:S(2)}) async-start(f32[32,16,128]{2,1,0:T(8,128)} %shard_map.202), calls=%async_computation.1 | async-start | bytes 524288 | tf_op jit(solution)/shard_map/all_to_all | solution.py:153
  20.1 14.2 %collective-permute-start = (bf16[128,256]{1,0:T(8,128)(2,1)}, bf16[128,256]{1,0:T(8,128)(2,1)S(1)}, u32[]{:S(2)}, u32[]{:S(2)}) collective-permute-start(bf16[128,256]{1,0:T(8,128)(2,1)} %param.18), channel_id=1, source_target_pairs={{0,8},{8,0},{1,9},{9,1},{2,10},{10,2},{3,11},{11,3},{4,12},{12,4},... | collective-permute-start | bytes 196616 | tf_op jit(solution)/shard_map/ppermute | solution.py:149
  34.4 43.1 %copy-start.4 = (bf16[256,256]{1,0:T(8,128)(2,1)S(1)}, bf16[256,256]{1,0:T(8,128)(2,1)}, u32[]{:S(2)}) copy-start(bf16[256,256]{1,0:T(8,128)(2,1)} %constant.31.clone.ll) | copy-start | bytes 393220
  34.4 43.1 %copy-start.5 = (f32[256,128]{1,0:T(8,128)S(1)}, f32[256,128]{1,0:T(8,128)}, u32[]{:S(2)}) copy-start(f32[256,128]{1,0:T(8,128)} %constant.36.clone.tr) | copy-start | bytes 393220
  35.3 42.2 %copy-start.1 = (bf16[512,256]{1,0:T(8,128)(2,1)S(1)}, bf16[512,256]{1,0:T(8,128)(2,1)}, u32[]{:S(2)}) copy-start(bf16[512,256]{1,0:T(8,128)(2,1)} %constant.28.clone.rh) | copy-start | bytes 786436
  35.3 42.2 %copy-start.2 = (bf16[512,256]{1,0:T(8,128)(2,1)S(1)}, bf16[512,256]{1,0:T(8,128)(2,1)}, u32[]{:S(2)}) copy-start(bf16[512,256]{1,0:T(8,128)(2,1)} %constant.29.clone.rl) | copy-start | bytes 786436
  35.3 42.2 %copy-start.3 = (bf16[256,256]{1,0:T(8,128)(2,1)S(1)}, bf16[256,256]{1,0:T(8,128)(2,1)}, u32[]{:S(2)}) copy-start(bf16[256,256]{1,0:T(8,128)(2,1)} %constant.30.clone.lh) | copy-start | bytes 393220
  46.6 7.5 %collective-permute-start.1 = (bf16[4,2,128,256]{3,2,1,0:T(8,128)(2,1)S(1)}, bf16[4,2,128,256]{3,2,1,0:T(8,128)(2,1)S(1)}, u32[]{:S(2)}, u32[]{:S(2)}) collective-permute-start(bf16[4,2,128,256]{3,2,1,0:T(8,128)(2,1)S(1)} %bitcast.6), channel_id=1, source_target_pairs={{0,1},{1,0},{2,3},{3,2},{4,5},{5,4},{6,7},{7,6},{8,9},{9,8},{10,11... | collective-permute-start | bytes 1572872 | tf_op jit(solution)/shard_map/ppermute | solution.py:156
  54.2 1.6 %copy-start = (bf16[4096,256]{1,0:T(8,128)(2,1)S(1)}, bf16[4096,256]{1,0:T(8,128)(2,1)}, u32[]{:S(2)}) copy-start(bf16[4096,256]{1,0:T(8,128)(2,1)} %proj_ref.1) | copy-start | bytes 6291460
  55.7 0.8 copy-start.16
  56.6 0.8 copy-start.17
  57.4 31.8 %copy-start.7 = (bf16[256,512]{1,0:T(8,128)(2,1)S(1)}, bf16[256,512]{1,0:T(8,128)(2,1)}, u32[]{:S(2)}) copy-start(bf16[256,512]{1,0:T(8,128)(2,1)} %constant.32.clone.rth) | copy-start | bytes 786436
  57.4 31.8 %copy-start.8 = (bf16[256,512]{1,0:T(8,128)(2,1)S(1)}, bf16[256,512]{1,0:T(8,128)(2,1)}, u32[]{:S(2)}) copy-start(bf16[256,512]{1,0:T(8,128)(2,1)} %constant.33.clone.rtl) | copy-start | bytes 786436
  57.4 31.8 %copy-start.14 = (bf16[256,256]{1,0:T(8,128)(2,1)S(1)}, bf16[256,256]{1,0:T(8,128)(2,1)}, u32[]{:S(2)}) copy-start(bf16[256,256]{1,0:T(8,128)(2,1)} %constant.34.clone.lth) | copy-start | bytes 393220
  57.4 31.8 %copy-start.15 = (bf16[256,256]{1,0:T(8,128)(2,1)S(1)}, bf16[256,256]{1,0:T(8,128)(2,1)}, u32[]{:S(2)}) copy-start(bf16[256,256]{1,0:T(8,128)(2,1)} %constant.35.clone.ltl) | copy-start | bytes 393220
  59.2 30.0 %all-to-all-start = ((f32[32,8,128]{2,1,0:T(8,128)}), f32[32,8,128]{2,1,0:T(8,128)S(1)}, u32[]{:S(2)}, u32[]{:S(2)}) async-start(f32[32,8,128]{2,1,0:T(8,128)} %get-tuple-element.11), calls=%async_computation | async-start | bytes 262144 | tf_op jit(solution)/shard_map/all_to_all | solution.py:164
  79.0 37.5 %copy-start.10 = (bf16[128,256]{1,0:T(8,128)(2,1)S(1)}, bf16[128,256]{1,0:T(8,128)(2,1)}, u32[]{:S(2)}) copy-start(bf16[128,256]{1,0:T(8,128)(2,1)} %keys_ref.3) | copy-start | bytes 196612
  79.0 37.5 %copy-start.12 = (bf16[128,256]{1,0:T(8,128)(2,1)S(1)}, bf16[128,256]{1,0:T(8,128)(2,1)}, u32[]{:S(2)}) copy-start(bf16[128,256]{1,0:T(8,128)(2,1)} %values_ref.3) | copy-start | bytes 196612
  79.0 37.5 %copy-start.18 = (f32[256]{0:T(256)S(1)}, f32[256]{0:T(256)}, u32[]{:S(2)}) copy-start(f32[256]{0:T(256)} %param.25) | copy-start | bytes 3076

commit v2 on v1

--- a/solution.py
+++ b/solution.py
@@ -16,7 +16,8 @@
 TP = ("zh", "y", "core")
 VMEM = pl.BlockSpec(memory_space=pltpu.VMEM)
 SMEM = pl.BlockSpec(memory_space=pltpu.SMEM)
-PARAMS = pltpu.CompilerParams(vmem_limit_bytes=48 * 1024 * 1024)
+HBM = pl.BlockSpec(memory_space=pltpu.HBM)
+PARAMS = pltpu.CompilerParams(vmem_limit_bytes=16 * 1024 * 1024)
 
 
 def split_table(table):
@@ -61,36 +62,74 @@
     return dot3(halves(turned), lane)
 
 
-def prep_kernel(scale, filter_ref, keys_ref, values_ref, out_ref):
+def fetch(pairs, sems):
+    copies = [pltpu.make_async_copy(src, dst, sems.at[i]) for i, (src, dst) in enumerate(pairs)]
+    for copy in copies:
+        copy.start()
+    return copies
+
+
+def prep_kernel(
+    scale, filter_hbm, keys_hbm, values_hbm, own_hbm, out_ref, own_ref, filter_ref, keys_ref, values_ref, sems
+):
+    pairs = [(filter_hbm, filter_ref), (keys_hbm, keys_ref), (values_hbm, values_ref), (own_hbm, own_ref)]
+    copies = fetch(pairs, sems)
     chans = out_ref.shape[1] // 2
     shape = (out_ref.shape[0], chans, out_ref.shape[2])
+    copies[0].wait()
     out_ref[:, :chans, :] = (filter_ref[...] * scale).T.reshape(shape)
+    copies[1].wait()
+    copies[2].wait()
     gated = keys_ref[...].astype(F32) * values_ref[...].astype(F32)
     out_ref[:, chans:, :] = gated.T.reshape(shape)
-
-
-def matmul_kernel(place_ref, near_ref, far_ref, proj_ref, queries_ref, conv_ref, grad_q_ref, grad_ref, turned_ref):
-    n_y, n_zh, _, width = near_ref.shape
-    zh, core = place_ref[0], place_ref[1]
-    total = jnp.zeros(grad_ref.shape, F32)
-    for ref, which in ((near_ref, 0), (far_ref, 1)):
-        for y in range(n_y):
-            for other in range(n_zh):
-                part = ((zh ^ other) * n_y + y) * 2 + (core ^ which)
-                weights = proj_ref[pl.ds(pl.multiple_of(part * width, width), width), :]
-                total += jnp.dot(ref[y, other], weights, preferred_element_type=F32)
-    grad_q_ref[...] = (total * conv_ref[...].astype(F32)).astype(BF16)
-    grad = total * queries_ref[...].astype(F32)
-    grad_ref[...] = grad
-    turned_ref[...] = grad.T.reshape(turned_ref.shape)
-
-
-def spectra_kernel(x_ref, rh, rl, lh, ll, tr, ti, out_ref):
+    copies[3].wait()
+
+
+def join_kernel(place_ref, own_ref, far_ref, out_ref):
+    zh = place_ref[0]
+    out_ref[zh] = own_ref[...]
+    out_ref[1 - zh] = far_ref[...]
+
+
+def products(given_ref, proj_ref):
+    n_y, n_zh = given_ref.shape[:2]
+    total = None
+    for y in range(n_y):
+        for zh in range(n_zh):
+            term = jnp.dot(given_ref[y, zh], proj_ref[zh * n_y + y], preferred_element_type=F32)
+            total = term if total is None else total + term
+    return total
+
+
+def near_kernel(
+    place_ref, near_ref, x_ref, rh, rl, lh, ll, tr, ti, proj_hbm, queries_hbm, conv_hbm,
+    part_ref, spec_ref, far_proj_ref, queries_ref, conv_ref, near_proj_ref, sems,
+):
+    core = place_ref[1]
+    pairs = [
+        (proj_hbm.at[:, core], near_proj_ref),
+        (proj_hbm.at[:, 1 - core], far_proj_ref),
+        (queries_hbm, queries_ref),
+        (conv_hbm, conv_ref),
+    ]
+    copies = fetch(pairs, sems)
     blocks, both, lanes = x_ref.shape
     chans = both // 2
     for field in range(2):
         x = x_ref[:, field * chans : (field + 1) * chans, :].reshape(blocks * chans, lanes)
-        out_ref[field] = forward(x, (rh[...], rl[...]), (lh[...], ll[...]), tr[...], ti[...])
+        spec_ref[field] = forward(x, (rh[...], rl[...]), (lh[...], ll[...]), tr[...], ti[...])
+    copies[0].wait()
+    part_ref[...] = products(near_ref, near_proj_ref)
+    for copy in copies[1:]:
+        copy.wait()
+
+
+def far_kernel(far_ref, part_ref, proj_ref, queries_ref, conv_ref, grad_q_ref, grad_ref, turned_ref):
+    total = part_ref[...] + products(far_ref, proj_ref)
+    grad = total * queries_ref[...].astype(F32)
+    turned_ref[...] = grad.T.reshape(turned_ref.shape)
+    grad_ref[...] = grad
+    grad_q_ref[...] = (total * conv_ref[...].astype(F32)).astype(BF16)
 
 
 def correlate_kernel(scale, x_ref, spec_ref, rh, rl, lh, ll, rth, rtl, lth, ltl, tr, ti, out_ref):
@@ -123,57 +162,83 @@
     filter_grad_ref[...] = x_ref[:, chans:, :].reshape(blocks * chans, lanes).T * scale
 
 
-def call(kernel, outs, n_in, scalars=0):
-    return pl.pallas_call(
+def call(kernel, outs, specs, scratch=(), cost=None):
+    run = pl.pallas_call(
         kernel,
         out_shape=outs,
-        in_specs=[SMEM] * scalars + [VMEM] * (n_in - scalars),
+        in_specs=specs,
         out_specs=jax.tree.map(lambda _: VMEM, outs),
+        scratch_shapes=scratch,
         compiler_params=PARAMS,
+        cost_estimate=cost,
     )
+
+    def held(x, spec):
+        return pltpu.with_memory_space_constraint(x, pltpu.HBM) if spec is HBM else x
+
+    return lambda *args: run(*map(held, args, specs))
 
 
 def body(out_grad, out_proj, queries, keys, values, conv_out, long_filter, skip_gain):
     tok, width = queries.shape
     n_ctx = lax.axis_size("x") * lax.axis_size("zl")
+    n_half = lax.axis_size("zh") * lax.axis_size("y")
     chans = width // n_ctx
     total_len = tok * n_ctx
     inv_root = 1.0 / math.sqrt(total_len)
     shape = jax.ShapeDtypeStruct
+    dma = pltpu.SemaphoreType.DMA
 
     rows, lane, twist_re, twist_im = tables(n_ctx, tok, chans)
     fwd = [jnp.asarray(t) for t in (*split_table(rows), *split_table(lane))]
     inv = [jnp.asarray(t) for t in (*split_table(rows.T), *split_table(lane.T))]
     twist = [jnp.asarray(twist_re), jnp.asarray(twist_im)]
+    place = jnp.stack([lax.axis_index("zh"), lax.axis_index("core")]).astype(jnp.int32)
 
     far = lax.ppermute(out_grad, "zh", [(0, 1), (1, 0)])
-    prepared = call(functools.partial(prep_kernel, inv_root), shape((n_ctx, 2 * chans, tok), F32), 3)(
-        long_filter, keys, values
-    )
+    block = shape((tok, width), BF16)
+    prepared, own = call(
+        functools.partial(prep_kernel, inv_root),
+        (shape((n_ctx, 2 * chans, tok), F32), block),
+        [HBM] * 4,
+        [pltpu.VMEM((tok, width), F32), pltpu.VMEM((tok, width), BF16), pltpu.VMEM((tok, width), BF16), dma((4,))],
+    )(long_filter, keys, values, out_grad)
     fields = lax.all_to_all(prepared, CTX, 0, 0)
 
-    near = lax.all_gather(jnp.stack([out_grad, far]), "y")
+    joined = call(
+        join_kernel,
+        shape((2, tok, width), BF16),
+        [SMEM, VMEM, VMEM],
+        cost=pl.CostEstimate(flops=COST, bytes_accessed=1 << 20, transcendentals=0),
+    )(place, own, far)
+    near = lax.all_gather(joined, "y")
     across = lax.ppermute(near, "core", [(0, 1), (1, 0)])
-    place = jnp.stack([lax.axis_index("zh"), lax.axis_index("core")]).astype(jnp.int32)
+    half = shape((n_half, width, width), BF16)
+    part, spec, far_proj, gate, saved = call(
+        near_kernel,
+        (shape((tok, width), F32), shape((2, n_ctx * chans, 2 * tok), F32), half, block, block),
+        [SMEM] + [VMEM] * 8 + [HBM] * 3,
+        [pltpu.VMEM(half.shape, BF16), dma((4,))],
+    )(place, near, fields, *fwd, *twist, out_proj.reshape(n_half, 2, width, width), queries, conv_out)
+    across, part = lax.optimization_barrier((across, part))
     grad_q, grad, turned = call(
-        matmul_kernel,
-        (shape((tok, width), BF16), shape((tok, width), F32), shape((n_ctx, chans, tok), F32)),
-        6,
-        1,
-    )(place, near, across, out_proj, queries, conv_out)
+        far_kernel, (block, shape((tok, width), F32), shape((n_ctx, chans, tok), F32)), [VMEM] * 5
+    )(across, part, far_proj, gate, saved)
     turned = lax.all_to_all(turned, CTX, 0, 0)
 
-    spec = call(spectra_kernel, shape((2, n_ctx * chans, 2 * tok), F32), 7)(fields, *fwd, *twist)
     corr = call(
-        functools.partial(correlate_kernel, 1.0 / total_len), shape((n_ctx, 2 * chans, tok), F32), 12
+        functools.partial(correlate_kernel, 1.0 / total_len), shape((n_ctx, 2 * chans, tok), F32), [VMEM] * 12
     )(turned, spec, *fwd, *inv, *twist)
     corr = lax.all_to_all(corr, CTX, 0, 0)
     grad_k, grad_v, filter_grad = call(
         functools.partial(final_kernel, inv_root),
         (shape((tok, width), BF16), shape((tok, width), BF16), shape((tok, width), F32)),
-        5,
+        [VMEM] * 5,
     )(corr, grad, keys, values, skip_gain[None, :])
     return grad_q, grad_k, grad_v, filter_grad
+
+
+COST = 1 << 35
 
 
 def solution(mesh):

time: 118 us -> 101 us (0.86)
  the two profiles are of different devices: /device:TPU:1 before, /device:TPU:8 now
where the time goes in v2:
time: 101 us
  blocking collectives  61.9 us (61%)
  starting transfers between devices  25.5 us (25%)
  Pallas kernels  9.12 us (9%)
  waiting for transfers between devices  3.11 us (3%)
    all_to_all x1, blocking collectives, body(): turned = lax.all_to_all(turned, CTX, 0, 0)  24.4 us
    all_to_all x1, blocking collectives, body(): corr = lax.all_to_all(corr, CTX, 0, 0)  24 us
    ppermute x1, starting transfers between devices, body(): far = lax.ppermute(out_grad, 'zh', [(0, 1), (1, 0)])  15.7 us
    all_gather x1, blocking collectives, body(): near = lax.all_gather(joined, 'y')  13.5 us
    pallas_call x6, Pallas kernels, call(): return lambda *args: run(*map(held, args, specs))  9.12 us
    all_to_all x1, starting transfers between devices, body(): fields = lax.all_to_all(prepared, CTX, 0, 0)  7.89 us
    all_to_all x1, waiting for transfers between devices, body(): fields = lax.all_to_all(prepared, CTX, 0, 0)  3.11 us
  transfers between devices with their start and end apart: 3, of which 1 were waited for; matrix products, arithmetic and copies ran while one was open for 0% of the time, Pallas kernels for 6%

profile of v2, /device:TPU:8, one launch (start us, length us, event | category | flops | bytes accessed | tf_op | source)
XLA Modules:
  0.0 100.6 jit_solution(10240088623891643289)
XLA Ops:
  0.6 15.7 %collective-permute-start = (bf16[128,256]{1,0:T(8,128)(2,1)}, bf16[128,256]{1,0:T(8,128)(2,1)S(1)}, u32[]{:S(2)}, u32[]{:S(2)}) collective-permute-start(bf16[128,256]{1,0:T(8,128)(2,1)} %own_hbm.1), channel_id=1, source_target_pairs={{0,8},{8,0},{1,9},{9,1},{2,10},{10,2},{3,11},{11,3},{4,12},{12,4},... | collective-permute-start | bytes 196616 | tf_op jit(solution)/shard_map/ppermute | solution.py:198
  16.4 1.8 %shard_map.201 = (f32[32,16,128]{2,1,0:T(8,128)}, bf16[128,256]{1,0:T(8,128)(2,1)S(1)}) custom-call(f32[128,256]{1,0:T(8,128)} %filter_hbm.1, bf16[128,256]{1,0:T(8,128)(2,1)} %keys_ref.1, bf16[128,256]{1,0:T(8,128)(2,1)} %values_ref.1, bf16[128,256]{1,0:T(8,128)(2,1)} %own_hbm.1), custom_call_target="tpu_custom_call" | custom-call | tf_op jit(solution)/shard_map/pallas_call | solution.py:179
  18.2 7.9 %all-to-all-start = ((f32[32,16,128]{2,1,0:T(8,128)}), f32[32,16,128]{2,1,0:T(8,128)S(1)}, u32[]{:S(2)}, u32[]{:S(2)}) async-start(f32[32,16,128]{2,1,0:T(8,128)} %get-tuple-element.20), calls=%async_computation | async-start | bytes 524288 | tf_op jit(solution)/shard_map/all_to_all | solution.py:206
  26.1 0.1 pad_add_fusion.place_ref
  26.2 0.0 collective-permute-done.far_ref
  26.2 0.0 copy-start.3
  26.2 0.0 copy-start.4
  26.2 0.0 copy-start.5
  26.2 0.6 shard_map.202
  26.8 13.5 %all-gather = bf16[8,128,256]{2,1,0:T(8,128)(2,1)S(1)} all-gather(bf16[2,128,256]{2,1,0:T(8,128)(2,1)S(1)} %shard_map.202), channel_id=2, replica_groups=mesh['x'=4,'zl'=8,'zh'=2,'y'=4,'core'=2] {'y'}, dimensions={0}, use_global_device_ids=true | all-gather | bytes 655360 | tf_op jit(solution)/shard_map/all_gather | solution.py:214
  40.3 1.9 %collective-permute-start.1 = (bf16[4,2,128,256]{3,2,1,0:T(8,128)(2,1)S(1)}, bf16[4,2,128,256]{3,2,1,0:T(8,128)(2,1)S(1)}, u32[]{:S(2)}, u32[]{:S(2)}) collective-permute-start(bf16[4,2,128,256]{3,2,1,0:T(8,128)(2,1)S(1)} %bitcast.5), channel_id=1, source_target_pairs={{0,1},{1,0},{2,3},{3,2},{4,5},{5,4},{6,7},{7,6},{8,9},{9,8},{10,11... | collective-permute-start | bytes 1572872 | tf_op jit(solution)/shard_map/ppermute | solution.py:215
  42.3 3.1 %all-to-all-done.x_ref = f32[32,16,128]{2,1,0:T(8,128)S(1)} async-done(((f32[32,16,128]{2,1,0:T(8,128)}), f32[32,16,128]{2,1,0:T(8,128)S(1)}, u32[]{:S(2)}, u32[]{:S(2)}) %all-to-all-start) | async-done | bytes 262176 | tf_op jit(solution)/shard_map/all_to_all | solution.py:206
  45.4 0.0 copy-done
  45.4 0.0 copy-done.1
  45.4 0.0 copy-done.2
  45.4 0.0 copy-done.3
  45.4 0.0 copy-done.4
  45.4 0.0 copy-done.5
  45.4 0.0 copy-start.8
  45.4 0.0 copy-start.9
  45.4 0.0 copy-start.10
  45.4 0.0 copy-start.11
  45.5 3.3 %shard_map.203 = (f32[128,256]{1,0:T(8,128)S(1)}, f32[2,256,256]{2,1,0:T(8,128)S(1)}, bf16[8,256,256]{2,1,0:T(8,128)(2,1)S(1)}, bf16[128,256]{1,0:T(8,128)(2,1)S(1)}, bf16[128,256]{1,0:T(8,128)(2,1)S(1)}) custom-call(s32[2]{0:T(128)S(1)} %pad_add_fusion.place_ref, bf16[4,2,128,256]{3,2,1,0:T(8,128)(2,1)S(1)} %bitcast.6, ...), custom_call_target="tpu_custom_call" | custom-call | tf_op jit(solution)/shard_map/pallas_call | solution.py:179
  48.8 0.0 collective-permute-done.1.far_ref
  48.8 1.0 shard_map.204
  49.8 24.4 %all_to_all.15.x_ref = f32[32,8,128]{2,1,0:T(8,128)S(1)} all-to-all(f32[32,8,128]{2,1,0:T(8,128)S(1)} %get-tuple-element.28), channel_id=1, replica_groups=mesh['x'=4,'zl'=8,'zh'=2,'y'=4,'core'=2] {'x','zl'}, dimensions={0} | all-to-all | bytes 262144 | tf_op jit(solution)/shard_map/all_to_all | solution.py:227
  74.1 0.0 copy-done.8
  74.1 0.0 copy-done.9
  74.2 1.6 %shard_map.205 = f32[32,16,128]{2,1,0:T(8,128)S(1)} custom-call(f32[32,8,128]{2,1,0:T(8,128)S(1)} %all_to_all.15.x_ref, f32[2,256,256]{2,1,0:T(8,128)S(1)} %get-tuple-element.29.spec_ref, bf16[512,256]{1,0:T(8,128)(2,1)S(1)} %copy-done, bf16[512,256]{1,0:T(8,128)(2,1)S(1)} %copy-done.1, bf16[256,256]{1,0:T(8,128)(2,1)S(1)} %copy-done.2, ...), custom_call_target="tpu_custom_call" | custom-call | tf_op jit(solution)/shard_map/pallas_call | solution.py:179
  75.8 24.0 %all_to_all.16.x_ref = f32[32,16,128]{2,1,0:T(8,128)S(1)} all-to-all(f32[32,16,128]{2,1,0:T(8,128)S(1)} %shard_map.205), channel_id=1, replica_groups=mesh['x'=4,'zl'=8,'zh'=2,'y'=4,'core'=2] {'x','zl'}, dimensions={0} | all-to-all | bytes 524288 | tf_op jit(solution)/shard_map/all_to_all | solution.py:232
  99.8 0.0 copy-done.7
  99.8 0.8 shard_map.206
  (10 shorter events, 0.0 us)
Async XLA Ops:
  0.6 25.6 %collective-permute-start = (bf16[128,256]{1,0:T(8,128)(2,1)}, bf16[128,256]{1,0:T(8,128)(2,1)S(1)}, u32[]{:S(2)}, u32[]{:S(2)}) collective-permute-start(bf16[128,256]{1,0:T(8,128)(2,1)} %own_hbm.1), channel_id=1, source_target_pairs={{0,8},{8,0},{1,9},{9,1},{2,10},{10,2},{3,11},{11,3},{4,12},{12,4},... | collective-permute-start | bytes 196616 | tf_op jit(solution)/shard_map/ppermute | solution.py:198
  18.2 27.1 %all-to-all-start = ((f32[32,16,128]{2,1,0:T(8,128)}), f32[32,16,128]{2,1,0:T(8,128)S(1)}, u32[]{:S(2)}, u32[]{:S(2)}) async-start(f32[32,16,128]{2,1,0:T(8,128)} %get-tuple-element.20), calls=%async_computation | async-start | bytes 524288 | tf_op jit(solution)/shard_map/all_to_all | solution.py:206
  26.2 19.2 %copy-start = (bf16[512,256]{1,0:T(8,128)(2,1)S(1)}, bf16[512,256]{1,0:T(8,128)(2,1)}, u32[]{:S(2)}) copy-start(bf16[512,256]{1,0:T(8,128)(2,1)} %constant.28.clone.rh) | copy-start | bytes 786436
  26.2 19.2 %copy-start.1 = (bf16[512,256]{1,0:T(8,128)(2,1)S(1)}, bf16[512,256]{1,0:T(8,128)(2,1)}, u32[]{:S(2)}) copy-start(bf16[512,256]{1,0:T(8,128)(2,1)} %constant.29.clone.rl) | copy-start | bytes 786436
  26.2 19.2 %copy-start.2 = (bf16[256,256]{1,0:T(8,128)(2,1)S(1)}, bf16[256,256]{1,0:T(8,128)(2,1)}, u32[]{:S(2)}) copy-start(bf16[256,256]{1,0:T(8,128)(2,1)} %constant.30.clone.lh) | copy-start | bytes 393220
  26.2 19.2 %copy-start.3 = (bf16[256,256]{1,0:T(8,128)(2,1)S(1)}, bf16[256,256]{1,0:T(8,128)(2,1)}, u32[]{:S(2)}) copy-start(bf16[256,256]{1,0:T(8,128)(2,1)} %constant.31.clone.ll) | copy-start | bytes 393220
  26.2 19.2 %copy-start.4 = (f32[256,128]{1,0:T(8,128)S(1)}, f32[256,128]{1,0:T(8,128)}, u32[]{:S(2)}) copy-start(f32[256,128]{1,0:T(8,128)} %constant.36.clone.tr) | copy-start | bytes 393220
  26.2 19.2 %copy-start.5 = (f32[256,128]{1,0:T(8,128)S(1)}, f32[256,128]{1,0:T(8,128)}, u32[]{:S(2)}) copy-start(f32[256,128]{1,0:T(8,128)} %constant.37.clone.ti) | copy-start | bytes 393220
  40.3 8.5 %collective-permute-start.1 = (bf16[4,2,128,256]{3,2,1,0:T(8,128)(2,1)S(1)}, bf16[4,2,128,256]{3,2,1,0:T(8,128)(2,1)S(1)}, u32[]{:S(2)}, u32[]{:S(2)}) collective-permute-start(bf16[4,2,128,256]{3,2,1,0:T(8,128)(2,1)S(1)} %bitcast.5), channel_id=1, source_target_pairs={{0,1},{1,0},{2,3},{3,2},{4,5},{5,4},{6,7},{7,6},{8,9},{9,8},{10,11... | collective-permute-start | bytes 1572872 | tf_op jit(solution)/shard_map/ppermute | solution.py:215
  45.4 28.7 %copy-start.8 = (bf16[256,512]{1,0:T(8,128)(2,1)S(1)}, bf16[256,512]{1,0:T(8,128)(2,1)}, u32[]{:S(2)}) copy-start(bf16[256,512]{1,0:T(8,128)(2,1)} %constant.32.clone.rth) | copy-start | bytes 786436
  45.4 28.7 %copy-start.9 = (bf16[256,512]{1,0:T(8,128)(2,1)S(1)}, bf16[256,512]{1,0:T(8,128)(2,1)}, u32[]{:S(2)}) copy-start(bf16[256,512]{1,0:T(8,128)(2,1)} %constant.33.clone.rtl) | copy-start | bytes 786436
  45.4 28.7 %copy-start.10 = (bf16[256,256]{1,0:T(8,128)(2,1)S(1)}, bf16[256,256]{1,0:T(8,128)(2,1)}, u32[]{:S(2)}) copy-start(bf16[256,256]{1,0:T(8,128)(2,1)} %constant.34.clone.lth) | copy-start | bytes 393220
  45.4 28.7 %copy-start.11 = (bf16[256,256]{1,0:T(8,128)(2,1)S(1)}, bf16[256,256]{1,0:T(8,128)(2,1)}, u32[]{:S(2)}) copy-start(bf16[256,256]{1,0:T(8,128)(2,1)} %constant.35.clone.ltl) | copy-start | bytes 393220
  49.8 50.0 %copy-start.6 = (bf16[128,256]{1,0:T(8,128)(2,1)S(1)}, bf16[128,256]{1,0:T(8,128)(2,1)}, u32[]{:S(2)}) copy-start(bf16[128,256]{1,0:T(8,128)(2,1)} %keys_ref.1) | copy-start | bytes 196612
  49.8 50.0 %copy-start.7 = (bf16[128,256]{1,0:T(8,128)(2,1)S(1)}, bf16[128,256]{1,0:T(8,128)(2,1)}, u32[]{:S(2)}) copy-start(bf16[128,256]{1,0:T(8,128)(2,1)} %values_ref.1) | copy-start | bytes 196612
  49.8 50.0 %copy-start.12 = (f32[256]{0:T(256)S(1)}, f32[256]{0:T(256)}, u32[]{:S(2)}) copy-start(f32[256]{0:T(256)} %param.25) | copy-start | bytes 3076

commit v3 on v2

--- a/solution.py
+++ b/solution.py
@@ -17,6 +17,7 @@
 VMEM = pl.BlockSpec(memory_space=pltpu.VMEM)
 SMEM = pl.BlockSpec(memory_space=pltpu.SMEM)
 HBM = pl.BlockSpec(memory_space=pltpu.HBM)
+STRETCH = 2.0**17
 PARAMS = pltpu.CompilerParams(vmem_limit_bytes=16 * 1024 * 1024)
 
 
@@ -72,7 +73,12 @@
 def prep_kernel(
     scale, filter_hbm, keys_hbm, values_hbm, own_hbm, out_ref, own_ref, filter_ref, keys_ref, values_ref, sems
 ):
-    pairs = [(filter_hbm, filter_ref), (keys_hbm, keys_ref), (values_hbm, values_ref), (own_hbm, own_ref)]
+    pairs = [
+        (filter_hbm, filter_ref),
+        (keys_hbm, keys_ref),
+        (values_hbm, values_ref),
+        (own_hbm, own_ref),
+    ]
     copies = fetch(pairs, sems)
     chans = out_ref.shape[1] // 2
     shape = (out_ref.shape[0], chans, out_ref.shape[2])
@@ -91,48 +97,47 @@
     out_ref[1 - zh] = far_ref[...]
 
 
-def products(given_ref, proj_ref):
+def products(core, given_ref, proj_ref):
     n_y, n_zh = given_ref.shape[:2]
     total = None
     for y in range(n_y):
         for zh in range(n_zh):
-            term = jnp.dot(given_ref[y, zh], proj_ref[zh * n_y + y], preferred_element_type=F32)
+            part = zh * n_y + y
+            weights = proj_ref[part] if core is None else proj_ref[part, core]
+            term = jnp.dot(given_ref[y, zh], weights, preferred_element_type=F32)
             total = term if total is None else total + term
     return total
 
 
 def near_kernel(
-    place_ref, near_ref, x_ref, rh, rl, lh, ll, tr, ti, proj_hbm, queries_hbm, conv_hbm,
-    part_ref, spec_ref, far_proj_ref, queries_ref, conv_ref, near_proj_ref, sems,
+    place_ref, near_ref, proj_ref, queries_hbm, conv_hbm, part_ref, far_proj_ref, queries_ref, conv_ref, sems
 ):
     core = place_ref[1]
-    pairs = [
-        (proj_hbm.at[:, core], near_proj_ref),
-        (proj_hbm.at[:, 1 - core], far_proj_ref),
-        (queries_hbm, queries_ref),
-        (conv_hbm, conv_ref),
-    ]
-    copies = fetch(pairs, sems)
+    copies = fetch([(queries_hbm, queries_ref), (conv_hbm, conv_ref)], sems)
+    part_ref[...] = products(core, near_ref, proj_ref)
+    for i in range(proj_ref.shape[0]):
+        far_proj_ref[i] = proj_ref[i, 1 - core]
+    for copy in copies:
+        copy.wait()
+
+
+def spectra_kernel(x_ref, rh, rl, lh, ll, tr, ti, out_ref):
     blocks, both, lanes = x_ref.shape
     chans = both // 2
     for field in range(2):
         x = x_ref[:, field * chans : (field + 1) * chans, :].reshape(blocks * chans, lanes)
-        spec_ref[field] = forward(x, (rh[...], rl[...]), (lh[...], ll[...]), tr[...], ti[...])
-    copies[0].wait()
-    part_ref[...] = products(near_ref, near_proj_ref)
-    for copy in copies[1:]:
-        copy.wait()
+        out_ref[field] = forward(x, (rh[...], rl[...]), (lh[...], ll[...]), tr[...], ti[...])
 
 
 def far_kernel(far_ref, part_ref, proj_ref, queries_ref, conv_ref, grad_q_ref, grad_ref, turned_ref):
-    total = part_ref[...] + products(far_ref, proj_ref)
+    total = part_ref[...] + products(None, far_ref, proj_ref)
     grad = total * queries_ref[...].astype(F32)
     turned_ref[...] = grad.T.reshape(turned_ref.shape)
     grad_ref[...] = grad
     grad_q_ref[...] = (total * conv_ref[...].astype(F32)).astype(BF16)
 
 
-def correlate_kernel(scale, x_ref, spec_ref, rh, rl, lh, ll, rth, rtl, lth, ltl, tr, ti, out_ref):
+def correlate_kernel(scale, stretch, x_ref, spec_ref, rh, rl, lh, ll, rth, rtl, lth, ltl, tr, ti, out_ref):
     blocks, chans, lanes = x_ref.shape
     n = blocks * chans
     twist_re, twist_im = tr[...], ti[...]
@@ -146,20 +151,25 @@
         re, im = back[:, :lanes], back[:, lanes:]
         sides.append(jnp.concatenate([re * twist_re + im * twist_im, im * twist_re - re * twist_im], axis=0))
     result = dot3((rth[...], rtl[...]), halves(jnp.concatenate(sides, axis=1)))
-    for field in range(2):
-        out_ref[:, field * chans : (field + 1) * chans, :] = result[:, field * lanes : (field + 1) * lanes].reshape(
-            blocks, chans, lanes
-        )
-
-
-def final_kernel(scale, x_ref, grad_ref, keys_ref, values_ref, skip_ref, grad_k_ref, grad_v_ref, filter_grad_ref):
-    blocks, both, lanes = x_ref.shape
-    chans = both // 2
-    conv = x_ref[:, :chans, :].reshape(blocks * chans, lanes).T
+    conv, filter_grad = [result[:, f * lanes : (f + 1) * lanes].reshape(blocks, chans, lanes) for f in range(2)]
+    high, low = halves(conv)
+    stretched = filter_grad * stretch
+    cubed = stretched * stretched * stretched
+    out_ref[...] = jnp.concatenate([high.astype(F32), low.astype(F32), cubed], axis=1).astype(BF16)
+
+
+def final_kernel(shrink, x_ref, grad_ref, keys_ref, values_ref, skip_ref, grad_k_ref, grad_v_ref, filter_grad_ref):
+    blocks, rows, lanes = x_ref.shape
+    chans = rows // 3
+    x = x_ref[...].astype(F32)
+    conv = (x[:, :chans, :] + x[:, chans : 2 * chans, :]).reshape(blocks * chans, lanes).T
     input_grad = conv + skip_ref[...] * grad_ref[...]
     grad_k_ref[...] = (input_grad * values_ref[...].astype(F32)).astype(BF16)
     grad_v_ref[...] = (input_grad * keys_ref[...].astype(F32)).astype(BF16)
-    filter_grad_ref[...] = x_ref[:, chans:, :].reshape(blocks * chans, lanes).T * scale
+    cubed = x[:, 2 * chans :, :].reshape(blocks * chans, lanes)
+    size = jnp.exp2(jnp.log2(jnp.maximum(jnp.abs(cubed), 1e-37)) * (1.0 / 3.0)) * shrink
+    root = jnp.where(cubed < 0.0, -size, jnp.where(cubed > 0.0, size, 0.0))
+    filter_grad_ref[...] = root.T
 
 
 def call(kernel, outs, specs, scratch=(), cost=None):
@@ -197,6 +207,8 @@
 
     far = lax.ppermute(out_grad, "zh", [(0, 1), (1, 0)])
     block = shape((tok, width), BF16)
+    half = shape((n_half, width, width), BF16)
+    proj = out_proj.reshape(n_half, 2, width, width)
     prepared, own = call(
         functools.partial(prep_kernel, inv_root),
         (shape((n_ctx, 2 * chans, tok), F32), block),
@@ -213,25 +225,27 @@
     )(place, own, far)
     near = lax.all_gather(joined, "y")
     across = lax.ppermute(near, "core", [(0, 1), (1, 0)])
-    half = shape((n_half, width, width), BF16)
-    part, spec, far_proj, gate, saved = call(
+    part, far_proj, gate, saved = call(
         near_kernel,
-        (shape((tok, width), F32), shape((2, n_ctx * chans, 2 * tok), F32), half, block, block),
-        [SMEM] + [VMEM] * 8 + [HBM] * 3,
-        [pltpu.VMEM(half.shape, BF16), dma((4,))],
-    )(place, near, fields, *fwd, *twist, out_proj.reshape(n_half, 2, width, width), queries, conv_out)
+        (shape((tok, width), F32), half, block, block),
+        [SMEM, VMEM, VMEM, HBM, HBM],
+        [dma((2,))],
+    )(place, near, proj, queries, conv_out)
     across, part = lax.optimization_barrier((across, part))
     grad_q, grad, turned = call(
         far_kernel, (block, shape((tok, width), F32), shape((n_ctx, chans, tok), F32)), [VMEM] * 5
     )(across, part, far_proj, gate, saved)
     turned = lax.all_to_all(turned, CTX, 0, 0)
 
+    spec = call(spectra_kernel, shape((2, n_ctx * chans, 2 * tok), F32), [VMEM] * 7)(fields, *fwd, *twist)
     corr = call(
-        functools.partial(correlate_kernel, 1.0 / total_len), shape((n_ctx, 2 * chans, tok), F32), [VMEM] * 12
+        functools.partial(correlate_kernel, 1.0 / total_len, inv_root * STRETCH),
+        shape((n_ctx, 3 * chans, tok), BF16),
+        [VMEM] * 12,
     )(turned, spec, *fwd, *inv, *twist)
     corr = lax.all_to_all(corr, CTX, 0, 0)
     grad_k, grad_v, filter_grad = call(
-        functools.partial(final_kernel, inv_root),
+        functools.partial(final_kernel, 1.0 / STRETCH),
         (shape((tok, width), BF16), shape((tok, width), BF16), shape((tok, width), F32)),
         [VMEM] * 5,
     )(corr, grad, keys, values, skip_gain[None, :])

time: 101 us -> 96.6 us (0.956)
  blocking collectives: 61.9 us -> 34.9 us
  starting transfers between devices: 25.5 us -> 38 us
  waiting for transfers between devices: 3.11 us -> 13.5 us
    all_to_all x1 -> x0, blocking collectives: 24.4 us -> none  [body(): turned = lax.all_to_all(turned, CTX, 0, 0)]
    all_to_all x0 -> x1, waiting for transfers between devices: none -> 13.1 us  [body(): turned = lax.all_to_all(turned, CTX, 0, 0)]
    all_to_all x0 -> x1, starting transfers between devices: none -> 12.5 us  [body(): turned = lax.all_to_all(turned, CTX, 0, 0)]
    all_to_all x1, waiting for transfers between devices: 3.11 us -> 0.11 us  [body(): fields = lax.all_to_all(prepared, CTX, 0, 0)]
    all_to_all x1, blocking collectives: 24 us -> 21.3 us  [body(): corr = lax.all_to_all(corr, CTX, 0, 0)]
    pallas_call x6 -> x7, Pallas kernels: 9.12 us -> 8.77 us  [call(): return lambda *args: run(*map(held, args, specs))]
  transfers between devices with their start and end apart: 3 -> 4, of which waited for: 1 -> 3; matrix products, arithmetic and copies ran while one was open for 0% -> 0% of each run, Pallas kernels for 6% -> 7%
where the time goes in v3:
time: 96.6 us; the launch traced here: 96.2 us
  starting transfers between devices  38 us (39%)
  blocking collectives  34.9 us (36%)
  waiting for transfers between devices  13.5 us (14%)
  Pallas kernels  8.77 us (9%)
    all_to_all x1, blocking collectives, body(): corr = lax.all_to_all(corr, CTX, 0, 0)  21.3 us
    ppermute x1, starting transfers between devices, body(): far = lax.ppermute(out_grad, 'zh', [(0, 1), (1, 0)])  15.7 us
    all_gather x1, blocking collectives, body(): near = lax.all_gather(joined, 'y')  13.7 us
    all_to_all x1, waiting for transfers between devices, body(): turned = lax.all_to_all(turned, CTX, 0, 0)  13.1 us
    all_to_all x1, starting transfers between devices, body(): turned = lax.all_to_all(turned, CTX, 0, 0)  12.5 us
    pallas_call x7, Pallas kernels, call(): return lambda *args: run(*map(held, args, specs))  8.77 us
    all_to_all x1, starting transfers between devices, body(): fields = lax.all_to_all(prepared, CTX, 0, 0)  7.89 us
  transfers between devices with their start and end apart: 4, of which 3 were waited for; matrix products, arithmetic and copies ran while one was open for 0% of the time, Pallas kernels for 7%

profile of v3, /device:TPU:8, one launch (start us, length us, event | category | flops | bytes accessed | tf_op | source)
XLA Modules:
  0.0 96.2 jit_solution(8304716453675049080)
XLA Ops:
  0.6 15.7 %collective-permute-start = (bf16[128,256]{1,0:T(8,128)(2,1)}, bf16[128,256]{1,0:T(8,128)(2,1)S(1)}, u32[]{:S(2)}, u32[]{:S(2)}) collective-permute-start(bf16[128,256]{1,0:T(8,128)(2,1)} %own_hbm.1), channel_id=1, source_target_pairs={{0,8},{8,0},{1,9},{9,1},{2,10},{10,2},{3,11},{11,3},{4,12},{12,4},... | collective-permute-start | bytes 196616 | tf_op jit(solution)/shard_map/ppermute | solution.py:208
  16.4 1.8 %shard_map.201 = (f32[32,16,128]{2,1,0:T(8,128)}, bf16[128,256]{1,0:T(8,128)(2,1)S(1)}) custom-call(f32[128,256]{1,0:T(8,128)} %filter_hbm.1, bf16[128,256]{1,0:T(8,128)(2,1)} %keys_ref.1, bf16[128,256]{1,0:T(8,128)(2,1)} %values_ref.1, bf16[128,256]{1,0:T(8,128)(2,1)} %own_hbm.1), custom_call_target="tpu_custom_call" | custom-call | tf_op jit(solution)/shard_map/pallas_call | solution.py:189
  18.2 7.9 %all-to-all-start.1 = ((f32[32,16,128]{2,1,0:T(8,128)}), f32[32,16,128]{2,1,0:T(8,128)S(1)}, u32[]{:S(2)}, u32[]{:S(2)}) async-start(f32[32,16,128]{2,1,0:T(8,128)} %get-tuple-element.27), calls=%async_computation.1 | async-start | bytes 524288 | tf_op jit(solution)/shard_map/all_to_all | solution.py:218
  26.1 0.1 pad_add_fusion.place_ref
  26.2 0.0 collective-permute-done.far_ref
  26.2 0.6 shard_map.202
  26.8 13.7 %all-gather = bf16[8,128,256]{2,1,0:T(8,128)(2,1)S(1)} all-gather(bf16[2,128,256]{2,1,0:T(8,128)(2,1)S(1)} %shard_map.202), channel_id=2, replica_groups=mesh['x'=4,'zl'=8,'zh'=2,'y'=4,'core'=2] {'y'}, dimensions={0}, use_global_device_ids=true | all-gather | bytes 655360 | tf_op jit(solution)/shard_map/all_gather | solution.py:226
  40.4 1.9 %collective-permute-start.1 = (bf16[4,2,128,256]{3,2,1,0:T(8,128)(2,1)S(1)}, bf16[4,2,128,256]{3,2,1,0:T(8,128)(2,1)S(1)}, u32[]{:S(2)}, u32[]{:S(2)}) collective-permute-start(bf16[4,2,128,256]{3,2,1,0:T(8,128)(2,1)S(1)} %bitcast.6), channel_id=1, source_target_pairs={{0,1},{1,0},{2,3},{3,2},{4,5},{5,4},{6,7},{7,6},{8,9},{9,8},{10,11... | collective-permute-start | bytes 1572872 | tf_op jit(solution)/shard_map/ppermute | solution.py:227
  42.4 0.0 copy-start.1
  42.4 0.0 copy-start.2
  42.4 0.0 copy-start.3
  42.4 0.0 copy-start.4
  42.4 0.0 copy-start.5
  42.4 0.0 copy-start.6
  42.4 1.4 %shard_map.203 = (f32[128,256]{1,0:T(8,128)S(1)}, bf16[8,256,256]{2,1,0:T(8,128)(2,1)S(1)}, bf16[128,256]{1,0:T(8,128)(2,1)S(1)}, bf16[128,256]{1,0:T(8,128)(2,1)S(1)}) custom-call(s32[2]{0:T(128)S(1)} %pad_add_fusion.place_ref, bf16[4,2,128,256]{3,2,1,0:T(8,128)(2,1)S(1)} %bitcast.7, bf16[8,2,256,256]{3,2,1,0:T(8,128)(2,1)S(1)} %bitcast.5, ...), custom_call_target="tpu_custom_call" | custom-call | tf_op jit(solution)/shard_map/pallas_call | solution.py:189
  43.9 0.0 copy-start.9
  43.9 0.0 copy-start.10
  43.9 0.0 copy-start.11
  43.9 0.0 copy-start.12
  43.9 0.3 collective-permute-done.1.far_ref
  44.2 1.0 %shard_map.204 = (bf16[128,256]{1,0:T(8,128)(2,1)}, f32[128,256]{1,0:T(8,128)S(1)}, f32[32,8,128]{2,1,0:T(8,128)}) custom-call(bf16[4,2,128,256]{3,2,1,0:T(8,128)(2,1)S(1)} %collective-permute-done.1.far_ref, f32[128,256]{1,0:T(8,128)S(1)} %get-tuple-element.21.part_ref, bf16[8,256,256]{2,1,0:T(8,128)(2,1)S(1)} %get-tuple-element.22.proj_ref, ...), custom_call_target="tpu_custom_call" | custom-call | tf_op jit(solution)/shard_map/pallas_call | solution.py:189
  45.3 0.1 all-to-all-done.1.x_ref
  45.4 12.5 %all-to-all-start = ((f32[32,8,128]{2,1,0:T(8,128)}), f32[32,8,128]{2,1,0:T(8,128)S(1)}, u32[]{:S(2)}, u32[]{:S(2)}) async-start(f32[32,8,128]{2,1,0:T(8,128)} %get-tuple-element.26), calls=%async_computation | async-start | bytes 262144 | tf_op jit(solution)/shard_map/all_to_all | solution.py:238
  57.9 0.0 copy-start.7
  57.9 0.0 copy-start.8
  57.9 0.0 copy-start.13
  57.9 1.5 %shard_map.205.spec_ref = f32[2,256,256]{2,1,0:T(8,128)S(1)} custom-call(f32[32,16,128]{2,1,0:T(8,128)S(1)} %all-to-all-done.1.x_ref, bf16[512,256]{1,0:T(8,128)(2,1)S(1)} %copy-done.1, bf16[512,256]{1,0:T(8,128)(2,1)S(1)} %copy-done.2, bf16[256,256]{1,0:T(8,128)(2,1)S(1)} %copy-done.3, bf16[256,256]{1,0:T(8,128)(2,1)S(1)} %copy-done.4, ...), custom_call_target="tpu_custom_call" | custom-call | tf_op jit(solution)/shard_map/pallas_call | solution.py:189
  59.4 13.1 %all-to-all-done.x_ref = f32[32,8,128]{2,1,0:T(8,128)S(1)} async-done(((f32[32,8,128]{2,1,0:T(8,128)}), f32[32,8,128]{2,1,0:T(8,128)S(1)}, u32[]{:S(2)}, u32[]{:S(2)}) %all-to-all-start) | async-done | bytes 131104 | tf_op jit(solution)/shard_map/all_to_all | solution.py:238
  72.5 0.0 copy-done.11
  72.5 1.6 %shard_map.206 = bf16[32,24,128]{2,1,0:T(8,128)(2,1)S(1)} custom-call(f32[32,8,128]{2,1,0:T(8,128)S(1)} %all-to-all-done.x_ref, f32[2,256,256]{2,1,0:T(8,128)S(1)} %shard_map.205.spec_ref, bf16[512,256]{1,0:T(8,128)(2,1)S(1)} %copy-done.1, bf16[512,256]{1,0:T(8,128)(2,1)S(1)} %copy-done.2, bf16[256,256]{1,0:T(8,128)(2,1)S(1)} %copy-done.3, ...), custom_call_target="tpu_custom_call" | custom-call | tf_op jit(solution)/shard_map/pallas_call | solution.py:189
  74.2 21.3 %all_to_all.15.x_ref = bf16[32,24,128]{2,1,0:T(8,128)(2,1)S(1)} all-to-all(bf16[32,24,128]{2,1,0:T(8,128)(2,1)S(1)} %shard_map.206), channel_id=1, replica_groups=mesh['x'=4,'zl'=8,'zh'=2,'y'=4,'core'=2] {'x','zl'}, dimensions={0} | all-to-all | bytes 393216 | tf_op jit(solution)/shard_map/all_to_all | solution.py:246
  95.4 0.8 shard_map.207
  (14 shorter events, 0.0 us)
Async XLA Ops:
  0.6 25.6 %collective-permute-start = (bf16[128,256]{1,0:T(8,128)(2,1)}, bf16[128,256]{1,0:T(8,128)(2,1)S(1)}, u32[]{:S(2)}, u32[]{:S(2)}) collective-permute-start(bf16[128,256]{1,0:T(8,128)(2,1)} %own_hbm.1), channel_id=1, source_target_pairs={{0,8},{8,0},{1,9},{9,1},{2,10},{10,2},{3,11},{11,3},{4,12},{12,4},... | collective-permute-start | bytes 196616 | tf_op jit(solution)/shard_map/ppermute | solution.py:208
  18.2 27.1 %all-to-all-start.1 = ((f32[32,16,128]{2,1,0:T(8,128)}), f32[32,16,128]{2,1,0:T(8,128)S(1)}, u32[]{:S(2)}, u32[]{:S(2)}) async-start(f32[32,16,128]{2,1,0:T(8,128)} %get-tuple-element.27), calls=%async_computation.1 | async-start | bytes 524288 | tf_op jit(solution)/shard_map/all_to_all | solution.py:218
  26.2 16.2 %copy-start = (bf16[4096,256]{1,0:T(8,128)(2,1)S(1)}, bf16[4096,256]{1,0:T(8,128)(2,1)}, u32[]{:S(2)}) copy-start(bf16[4096,256]{1,0:T(8,128)(2,1)} %param.19) | copy-start | bytes 6291460
  40.4 3.8 %collective-permute-start.1 = (bf16[4,2,128,256]{3,2,1,0:T(8,128)(2,1)S(1)}, bf16[4,2,128,256]{3,2,1,0:T(8,128)(2,1)S(1)}, u32[]{:S(2)}, u32[]{:S(2)}) collective-permute-start(bf16[4,2,128,256]{3,2,1,0:T(8,128)(2,1)S(1)} %bitcast.6), channel_id=1, source_target_pairs={{0,1},{1,0},{2,3},{3,2},{4,5},{5,4},{6,7},{7,6},{8,9},{9,8},{10,11... | collective-permute-start | bytes 1572872 | tf_op jit(solution)/shard_map/ppermute | solution.py:227
  42.4 15.5 %copy-start.1 = (bf16[512,256]{1,0:T(8,128)(2,1)S(1)}, bf16[512,256]{1,0:T(8,128)(2,1)}, u32[]{:S(2)}) copy-start(bf16[512,256]{1,0:T(8,128)(2,1)} %constant.28.clone.rh) | copy-start | bytes 786436
  42.4 15.5 %copy-start.2 = (bf16[512,256]{1,0:T(8,128)(2,1)S(1)}, bf16[512,256]{1,0:T(8,128)(2,1)}, u32[]{:S(2)}) copy-start(bf16[512,256]{1,0:T(8,128)(2,1)} %constant.29.clone.rl) | copy-start | bytes 786436
  42.4 15.5 %copy-start.3 = (bf16[256,256]{1,0:T(8,128)(2,1)S(1)}, bf16[256,256]{1,0:T(8,128)(2,1)}, u32[]{:S(2)}) copy-start(bf16[256,256]{1,0:T(8,128)(2,1)} %constant.30.clone.lh) | copy-start | bytes 393220
  42.4 15.5 %copy-start.4 = (bf16[256,256]{1,0:T(8,128)(2,1)S(1)}, bf16[256,256]{1,0:T(8,128)(2,1)}, u32[]{:S(2)}) copy-start(bf16[256,256]{1,0:T(8,128)(2,1)} %constant.31.clone.ll) | copy-start | bytes 393220
  42.4 15.5 %copy-start.5 = (f32[256,128]{1,0:T(8,128)S(1)}, f32[256,128]{1,0:T(8,128)}, u32[]{:S(2)}) copy-start(f32[256,128]{1,0:T(8,128)} %constant.36.clone.tr) | copy-start | bytes 393220
  42.4 15.5 %copy-start.6 = (f32[256,128]{1,0:T(8,128)S(1)}, f32[256,128]{1,0:T(8,128)}, u32[]{:S(2)}) copy-start(f32[256,128]{1,0:T(8,128)} %constant.37.clone.ti) | copy-start | bytes 393220
  43.9 28.7 %copy-start.9 = (bf16[256,512]{1,0:T(8,128)(2,1)S(1)}, bf16[256,512]{1,0:T(8,128)(2,1)}, u32[]{:S(2)}) copy-start(bf16[256,512]{1,0:T(8,128)(2,1)} %constant.32.clone.rth) | copy-start | bytes 786436
  43.9 28.6 %copy-start.10 = (bf16[256,512]{1,0:T(8,128)(2,1)S(1)}, bf16[256,512]{1,0:T(8,128)(2,1)}, u32[]{:S(2)}) copy-start(bf16[256,512]{1,0:T(8,128)(2,1)} %constant.33.clone.rtl) | copy-start | bytes 786436
  43.9 28.6 %copy-start.11 = (bf16[256,256]{1,0:T(8,128)(2,1)S(1)}, bf16[256,256]{1,0:T(8,128)(2,1)}, u32[]{:S(2)}) copy-start(bf16[256,256]{1,0:T(8,128)(2,1)} %constant.34.clone.lth) | copy-start | bytes 393220
  43.9 28.6 %copy-start.12 = (bf16[256,256]{1,0:T(8,128)(2,1)S(1)}, bf16[256,256]{1,0:T(8,128)(2,1)}, u32[]{:S(2)}) copy-start(bf16[256,256]{1,0:T(8,128)(2,1)} %constant.35.clone.ltl) | copy-start | bytes 393220
  45.4 27.2 %all-to-all-start = ((f32[32,8,128]{2,1,0:T(8,128)}), f32[32,8,128]{2,1,0:T(8,128)S(1)}, u32[]{:S(2)}, u32[]{:S(2)}) async-start(f32[32,8,128]{2,1,0:T(8,128)} %get-tuple-element.26), calls=%async_computation | async-start | bytes 262144 | tf_op jit(solution)/shard_map/all_to_all | solution.py:238
  57.9 37.5 %copy-start.7 = (bf16[128,256]{1,0:T(8,128)(2,1)S(1)}, bf16[128,256]{1,0:T(8,128)(2,1)}, u32[]{:S(2)}) copy-start(bf16[128,256]{1,0:T(8,128)(2,1)} %keys_ref.1) | copy-start | bytes 196612
  57.9 37.5 %copy-start.8 = (bf16[128,256]{1,0:T(8,128)(2,1)S(1)}, bf16[128,256]{1,0:T(8,128)(2,1)}, u32[]{:S(2)}) copy-start(bf16[128,256]{1,0:T(8,128)(2,1)} %values_ref.1) | copy-start | bytes 196612
  57.9 37.5 %copy-start.13 = (f32[256]{0:T(256)S(1)}, f32[256]{0:T(256)}, u32[]{:S(2)}) copy-start(f32[256]{0:T(256)} %param.25) | copy-start | bytes 3076

commit v4 on v3

--- a/solution.py
+++ b/solution.py
@@ -56,8 +56,10 @@
 
 
 def forward(x, rows, lane, twist_re, twist_im):
-    n = x.shape[0]
-    first = dot3(rows, halves(x))
+    n, lanes = x.shape
+    high, low = halves(x)
+    both = jnp.dot(rows[0], jnp.concatenate([high, low], axis=1), preferred_element_type=F32)
+    first = both[:, :lanes] + (both[:, lanes:] + jnp.dot(rows[1], high, preferred_element_type=F32))
     re, im = first[:n], first[n:]
     turned = jnp.concatenate([re * twist_re - im * twist_im, re * twist_im + im * twist_re], axis=1)
     return dot3(halves(turned), lane)
@@ -71,24 +73,27 @@
 
 
 def prep_kernel(
-    scale, filter_hbm, keys_hbm, values_hbm, own_hbm, out_ref, own_ref, filter_ref, keys_ref, values_ref, sems
+    scale, filter_hbm, keys_hbm, values_hbm, own_hbm,
+    out_hbm, own_ref, out_ref, filter_ref, keys_ref, values_ref, sems,
 ):
-    pairs = [
-        (filter_hbm, filter_ref),
-        (keys_hbm, keys_ref),
-        (values_hbm, values_ref),
-        (own_hbm, own_ref),
-    ]
-    copies = fetch(pairs, sems)
-    chans = out_ref.shape[1] // 2
-    shape = (out_ref.shape[0], chans, out_ref.shape[2])
+    copies = fetch(
+        [(keys_hbm, keys_ref), (values_hbm, values_ref), (filter_hbm, filter_ref), (own_hbm, own_ref)], sems
+    )
+    blocks, both, lanes = out_ref.shape
+    chans = both // 2
     copies[0].wait()
-    out_ref[:, :chans, :] = (filter_ref[...] * scale).T.reshape(shape)
     copies[1].wait()
+    gated = keys_ref[...].astype(F32) * values_ref[...].astype(F32)
+    out_ref[:, chans:, :] = gated.T.reshape(blocks, chans, lanes)
+    first = pltpu.make_async_copy(out_ref.at[:, chans:, :], out_hbm.at[:, chans:, :], sems.at[4])
+    first.start()
     copies[2].wait()
-    gated = keys_ref[...].astype(F32) * values_ref[...].astype(F32)
-    out_ref[:, chans:, :] = gated.T.reshape(shape)
+    out_ref[:, :chans, :] = (filter_ref[...] * scale).T.reshape(blocks, chans, lanes)
+    second = pltpu.make_async_copy(out_ref.at[:, :chans, :], out_hbm.at[:, :chans, :], sems.at[5])
+    second.start()
     copies[3].wait()
+    first.wait()
+    second.wait()
 
 
 def join_kernel(place_ref, own_ref, far_ref, out_ref):
@@ -172,12 +177,12 @@
     filter_grad_ref[...] = root.T
 
 
-def call(kernel, outs, specs, scratch=(), cost=None):
+def call(kernel, outs, specs, scratch=(), cost=None, out_specs=None):
     run = pl.pallas_call(
         kernel,
         out_shape=outs,
         in_specs=specs,
-        out_specs=jax.tree.map(lambda _: VMEM, outs),
+        out_specs=out_specs or jax.tree.map(lambda _: VMEM, outs),
         scratch_shapes=scratch,
         compiler_params=PARAMS,
         cost_estimate=cost,
@@ -205,7 +210,6 @@
     twist = [jnp.asarray(twist_re), jnp.asarray(twist_im)]
     place = jnp.stack([lax.axis_index("zh"), lax.axis_index("core")]).astype(jnp.int32)
 
-    far = lax.ppermute(out_grad, "zh", [(0, 1), (1, 0)])
     block = shape((tok, width), BF16)
     half = shape((n_half, width, width), BF16)
     proj = out_proj.reshape(n_half, 2, width, width)
@@ -213,8 +217,16 @@
         functools.partial(prep_kernel, inv_root),
         (shape((n_ctx, 2 * chans, tok), F32), block),
         [HBM] * 4,
-        [pltpu.VMEM((tok, width), F32), pltpu.VMEM((tok, width), BF16), pltpu.VMEM((tok, width), BF16), dma((4,))],
+        [
+            pltpu.VMEM((n_ctx, 2 * chans, tok), F32),
+            pltpu.VMEM((tok, width), F32),
+            pltpu.VMEM((tok, width), BF16),
+            pltpu.VMEM((tok, width), BF16),
+            dma((6,)),
+        ],
+        out_specs=(HBM, VMEM),
     )(long_filter, keys, values, out_grad)
+    far = lax.ppermute(own, "zh", [(0, 1), (1, 0)])
     fields = lax.all_to_all(prepared, CTX, 0, 0)
 
     joined = call(

time: 96.6 us -> 96.5 us (level)
  transfers between devices with their start and end apart: 4 -> 4, of which waited for: 3 -> 3; matrix products, arithmetic and copies ran while one was open for 0% -> 0% of each run, Pallas kernels for 7% -> 4%
where the time goes in v4:
time: 96.5 us; the launch traced here: 96.1 us
  starting transfers between devices  38 us (39%)
  blocking collectives  34.9 us (36%)
  waiting for transfers between devices  14.1 us (15%)
  Pallas kernels  8.07 us (8%)
    all_to_all x1, blocking collectives, body(): corr = lax.all_to_all(corr, CTX, 0, 0)  21.3 us
    ppermute x1, starting transfers between devices, body(): far = lax.ppermute(own, 'zh', [(0, 1), (1, 0)])  15.7 us
    all_gather x1, blocking collectives, body(): near = lax.all_gather(joined, 'y')  13.7 us
    all_to_all x1, waiting for transfers between devices, body(): turned = lax.all_to_all(turned, CTX, 0, 0)  13.7 us
    all_to_all x1, starting transfers between devices, body(): turned = lax.all_to_all(turned, CTX, 0, 0)  12.5 us
    pallas_call x7, Pallas kernels, call(): return lambda *args: run(*map(held, args, specs))  8.07 us
    all_to_all x1, starting transfers between devices, body(): fields = lax.all_to_all(prepared, CTX, 0, 0)  7.89 us
  transfers between devices with their start and end apart: 4, of which 3 were waited for; matrix products, arithmetic and copies ran while one was open for 0% of the time, Pallas kernels for 4%

profile of v4, /device:TPU:8, one launch (start us, length us, event | category | flops | bytes accessed | tf_op | source)
XLA Modules:
  0.0 96.1 jit_solution(1165593846825884390)
XLA Ops:
  0.6 1.8 %shard_map.201 = (f32[32,16,128]{2,1,0:T(8,128)}, bf16[128,256]{1,0:T(8,128)(2,1)S(1)}) custom-call(f32[128,256]{1,0:T(8,128)} %filter_hbm.1, bf16[128,256]{1,0:T(8,128)(2,1)} %keys_ref.1, bf16[128,256]{1,0:T(8,128)(2,1)} %values_ref.1, bf16[128,256]{1,0:T(8,128)(2,1)} %own_hbm.1), custom_call_target="tpu_custom_call" | custom-call | tf_op jit(solution)/shard_map/pallas_call | solution.py:194
  2.4 15.7 %collective-permute-start = (bf16[128,256]{1,0:T(8,128)(2,1)S(1)}, bf16[128,256]{1,0:T(8,128)(2,1)S(1)}, u32[]{:S(2)}, u32[]{:S(2)}) collective-permute-start(bf16[128,256]{1,0:T(8,128)(2,1)S(1)} %get-tuple-element.18.own_ref), channel_id=1, source_target_pairs={{0,8},{8,0},{1,9},{9,1},{2,10},{10,2},{3,11},{11,3},{4,12},{12,4},... | collective-permute-start | bytes 196616 | tf_op jit(solution)/shard_map/ppermute | solution.py:229
  18.1 7.9 %all-to-all-start.1 = ((f32[32,16,128]{2,1,0:T(8,128)}), f32[32,16,128]{2,1,0:T(8,128)S(1)}, u32[]{:S(2)}, u32[]{:S(2)}) async-start(f32[32,16,128]{2,1,0:T(8,128)} %get-tuple-element.27), calls=%async_computation.1 | async-start | bytes 524288 | tf_op jit(solution)/shard_map/all_to_all | solution.py:230
  26.0 0.1 pad_add_fusion.place_ref
  26.1 0.0 collective-permute-done.far_ref
  26.1 0.6 shard_map.202
  26.7 13.7 %all-gather = bf16[8,128,256]{2,1,0:T(8,128)(2,1)S(1)} all-gather(bf16[2,128,256]{2,1,0:T(8,128)(2,1)S(1)} %shard_map.202), channel_id=2, replica_groups=mesh['x'=4,'zl'=8,'zh'=2,'y'=4,'core'=2] {'y'}, dimensions={0}, use_global_device_ids=true | all-gather | bytes 655360 | tf_op jit(solution)/shard_map/all_gather | solution.py:238
  40.4 1.9 %collective-permute-start.1 = (bf16[4,2,128,256]{3,2,1,0:T(8,128)(2,1)S(1)}, bf16[4,2,128,256]{3,2,1,0:T(8,128)(2,1)S(1)}, u32[]{:S(2)}, u32[]{:S(2)}) collective-permute-start(bf16[4,2,128,256]{3,2,1,0:T(8,128)(2,1)S(1)} %bitcast.6), channel_id=1, source_target_pairs={{0,1},{1,0},{2,3},{3,2},{4,5},{5,4},{6,7},{7,6},{8,9},{9,8},{10,11... | collective-permute-start | bytes 1572872 | tf_op jit(solution)/shard_map/ppermute | solution.py:239
  42.3 0.0 copy-start.1
  42.3 0.0 copy-start.2
  42.3 0.0 copy-start.3
  42.3 0.0 copy-start.4
  42.3 0.0 copy-start.5
  42.4 0.0 copy-start.6
  42.4 1.4 %shard_map.203 = (f32[128,256]{1,0:T(8,128)S(1)}, bf16[8,256,256]{2,1,0:T(8,128)(2,1)S(1)}, bf16[128,256]{1,0:T(8,128)(2,1)S(1)}, bf16[128,256]{1,0:T(8,128)(2,1)S(1)}) custom-call(s32[2]{0:T(128)S(1)} %pad_add_fusion.place_ref, bf16[4,2,128,256]{3,2,1,0:T(8,128)(2,1)S(1)} %bitcast.7, bf16[8,2,256,256]{3,2,1,0:T(8,128)(2,1)S(1)} %bitcast.5, ...), custom_call_target="tpu_custom_call" | custom-call | tf_op jit(solution)/shard_map/pallas_call | solution.py:194
  43.8 0.0 copy-start.9
  43.8 0.0 copy-start.10
  43.8 0.0 copy-start.11
  43.8 0.0 copy-start.12
  43.9 0.3 collective-permute-done.1.far_ref
  44.2 1.0 %shard_map.204 = (bf16[128,256]{1,0:T(8,128)(2,1)}, f32[128,256]{1,0:T(8,128)S(1)}, f32[32,8,128]{2,1,0:T(8,128)}) custom-call(bf16[4,2,128,256]{3,2,1,0:T(8,128)(2,1)S(1)} %collective-permute-done.1.far_ref, f32[128,256]{1,0:T(8,128)S(1)} %get-tuple-element.21.part_ref, bf16[8,256,256]{2,1,0:T(8,128)(2,1)S(1)} %get-tuple-element.22.proj_ref, ...), custom_call_target="tpu_custom_call" | custom-call | tf_op jit(solution)/shard_map/pallas_call | solution.py:194
  45.2 0.1 all-to-all-done.1.x_ref
  45.3 12.5 %all-to-all-start = ((f32[32,8,128]{2,1,0:T(8,128)}), f32[32,8,128]{2,1,0:T(8,128)S(1)}, u32[]{:S(2)}, u32[]{:S(2)}) async-start(f32[32,8,128]{2,1,0:T(8,128)} %get-tuple-element.26), calls=%async_computation | async-start | bytes 262144 | tf_op jit(solution)/shard_map/all_to_all | solution.py:250
  57.8 0.0 copy-start.7
  57.9 0.0 copy-start.8
  57.9 0.0 copy-start.13
  57.9 0.9 shard_map.205.spec_ref
  58.8 13.7 %all-to-all-done.x_ref = f32[32,8,128]{2,1,0:T(8,128)S(1)} async-done(((f32[32,8,128]{2,1,0:T(8,128)}), f32[32,8,128]{2,1,0:T(8,128)S(1)}, u32[]{:S(2)}, u32[]{:S(2)}) %all-to-all-start) | async-done | bytes 131104 | tf_op jit(solution)/shard_map/all_to_all | solution.py:250
  72.5 0.0 copy-done.9
  72.5 1.5 %shard_map.206 = bf16[32,24,128]{2,1,0:T(8,128)(2,1)S(1)} custom-call(f32[32,8,128]{2,1,0:T(8,128)S(1)} %all-to-all-done.x_ref, f32[2,256,256]{2,1,0:T(8,128)S(1)} %shard_map.205.spec_ref, bf16[512,256]{1,0:T(8,128)(2,1)S(1)} %copy-done.1, bf16[512,256]{1,0:T(8,128)(2,1)S(1)} %copy-done.2, bf16[256,256]{1,0:T(8,128)(2,1)S(1)} %copy-done.3, ...), custom_call_target="tpu_custom_call" | custom-call | tf_op jit(solution)/shard_map/pallas_call | solution.py:194
  74.0 21.3 %all_to_all.15.x_ref = bf16[32,24,128]{2,1,0:T(8,128)(2,1)S(1)} all-to-all(bf16[32,24,128]{2,1,0:T(8,128)(2,1)S(1)} %shard_map.206), channel_id=1, replica_groups=mesh['x'=4,'zl'=8,'zh'=2,'y'=4,'core'=2] {'x','zl'}, dimensions={0} | all-to-all | bytes 393216 | tf_op jit(solution)/shard_map/all_to_all | solution.py:258
  95.3 0.8 shard_map.207
  (14 shorter events, 0.0 us)
Async XLA Ops:
  2.4 23.7 %collective-permute-start = (bf16[128,256]{1,0:T(8,128)(2,1)S(1)}, bf16[128,256]{1,0:T(8,128)(2,1)S(1)}, u32[]{:S(2)}, u32[]{:S(2)}) collective-permute-start(bf16[128,256]{1,0:T(8,128)(2,1)S(1)} %get-tuple-element.18.own_ref), channel_id=1, source_target_pairs={{0,8},{8,0},{1,9},{9,1},{2,10},{10,2},{3,11},{11,3},{4,12},{12,4},... | collective-permute-start | bytes 196616 | tf_op jit(solution)/shard_map/ppermute | solution.py:229
  18.1 27.2 %all-to-all-start.1 = ((f32[32,16,128]{2,1,0:T(8,128)}), f32[32,16,128]{2,1,0:T(8,128)S(1)}, u32[]{:S(2)}, u32[]{:S(2)}) async-start(f32[32,16,128]{2,1,0:T(8,128)} %get-tuple-element.27), calls=%async_computation.1 | async-start | bytes 524288 | tf_op jit(solution)/shard_map/all_to_all | solution.py:230
  26.1 16.2 %copy-start = (bf16[4096,256]{1,0:T(8,128)(2,1)S(1)}, bf16[4096,256]{1,0:T(8,128)(2,1)}, u32[]{:S(2)}) copy-start(bf16[4096,256]{1,0:T(8,128)(2,1)} %param.19) | copy-start | bytes 6291460
  40.4 3.8 %collective-permute-start.1 = (bf16[4,2,128,256]{3,2,1,0:T(8,128)(2,1)S(1)}, bf16[4,2,128,256]{3,2,1,0:T(8,128)(2,1)S(1)}, u32[]{:S(2)}, u32[]{:S(2)}) collective-permute-start(bf16[4,2,128,256]{3,2,1,0:T(8,128)(2,1)S(1)} %bitcast.6), channel_id=1, source_target_pairs={{0,1},{1,0},{2,3},{3,2},{4,5},{5,4},{6,7},{7,6},{8,9},{9,8},{10,11... | collective-permute-start | bytes 1572872 | tf_op jit(solution)/shard_map/ppermute | solution.py:239
  42.3 15.5 %copy-start.1 = (bf16[512,256]{1,0:T(8,128)(2,1)S(1)}, bf16[512,256]{1,0:T(8,128)(2,1)}, u32[]{:S(2)}) copy-start(bf16[512,256]{1,0:T(8,128)(2,1)} %constant.28.clone.rh) | copy-start | bytes 786436
  42.3 15.5 %copy-start.2 = (bf16[512,256]{1,0:T(8,128)(2,1)S(1)}, bf16[512,256]{1,0:T(8,128)(2,1)}, u32[]{:S(2)}) copy-start(bf16[512,256]{1,0:T(8,128)(2,1)} %constant.29.clone.rl) | copy-start | bytes 786436
  42.3 15.5 %copy-start.3 = (bf16[256,256]{1,0:T(8,128)(2,1)S(1)}, bf16[256,256]{1,0:T(8,128)(2,1)}, u32[]{:S(2)}) copy-start(bf16[256,256]{1,0:T(8,128)(2,1)} %constant.30.clone.lh) | copy-start | bytes 393220
  42.3 15.5 %copy-start.4 = (bf16[256,256]{1,0:T(8,128)(2,1)S(1)}, bf16[256,256]{1,0:T(8,128)(2,1)}, u32[]{:S(2)}) copy-start(bf16[256,256]{1,0:T(8,128)(2,1)} %constant.31.clone.ll) | copy-start | bytes 393220
  42.3 15.5 %copy-start.5 = (f32[256,128]{1,0:T(8,128)S(1)}, f32[256,128]{1,0:T(8,128)}, u32[]{:S(2)}) copy-start(f32[256,128]{1,0:T(8,128)} %constant.36.clone.tr) | copy-start | bytes 393220
  42.4 15.5 %copy-start.6 = (f32[256,128]{1,0:T(8,128)S(1)}, f32[256,128]{1,0:T(8,128)}, u32[]{:S(2)}) copy-start(f32[256,128]{1,0:T(8,128)} %constant.37.clone.ti) | copy-start | bytes 393220
  43.8 28.7 %copy-start.9 = (bf16[256,512]{1,0:T(8,128)(2,1)S(1)}, bf16[256,512]{1,0:T(8,128)(2,1)}, u32[]{:S(2)}) copy-start(bf16[256,512]{1,0:T(8,128)(2,1)} %constant.32.clone.rth) | copy-start | bytes 786436
  43.8 28.6 %copy-start.10 = (bf16[256,512]{1,0:T(8,128)(2,1)S(1)}, bf16[256,512]{1,0:T(8,128)(2,1)}, u32[]{:S(2)}) copy-start(bf16[256,512]{1,0:T(8,128)(2,1)} %constant.33.clone.rtl) | copy-start | bytes 786436
  43.8 28.6 %copy-start.11 = (bf16[256,256]{1,0:T(8,128)(2,1)S(1)}, bf16[256,256]{1,0:T(8,128)(2,1)}, u32[]{:S(2)}) copy-start(bf16[256,256]{1,0:T(8,128)(2,1)} %constant.34.clone.lth) | copy-start | bytes 393220
  43.8 28.6 %copy-start.12 = (bf16[256,256]{1,0:T(8,128)(2,1)S(1)}, bf16[256,256]{1,0:T(8,128)(2,1)}, u32[]{:S(2)}) copy-start(bf16[256,256]{1,0:T(8,128)(2,1)} %constant.35.clone.ltl) | copy-start | bytes 393220
  45.3 27.2 %all-to-all-start = ((f32[32,8,128]{2,1,0:T(8,128)}), f32[32,8,128]{2,1,0:T(8,128)S(1)}, u32[]{:S(2)}, u32[]{:S(2)}) async-start(f32[32,8,128]{2,1,0:T(8,128)} %get-tuple-element.26), calls=%async_computation | async-start | bytes 262144 | tf_op jit(solution)/shard_map/all_to_all | solution.py:250
  57.8 37.5 %copy-start.7 = (bf16[128,256]{1,0:T(8,128)(2,1)S(1)}, bf16[128,256]{1,0:T(8,128)(2,1)}, u32[]{:S(2)}) copy-start(bf16[128,256]{1,0:T(8,128)(2,1)} %keys_ref.1) | copy-start | bytes 196612
  57.9 37.5 %copy-start.8 = (bf16[128,256]{1,0:T(8,128)(2,1)S(1)}, bf16[128,256]{1,0:T(8,128)(2,1)}, u32[]{:S(2)}) copy-start(bf16[128,256]{1,0:T(8,128)(2,1)} %values_ref.1) | copy-start | bytes 196612
  57.9 37.4 %copy-start.13 = (f32[256]{0:T(256)S(1)}, f32[256]{0:T(256)}, u32[]{:S(2)}) copy-start(f32[256]{0:T(256)} %param.25) | copy-start | bytes 3076

commit v5 on v4

--- a/solution.py
+++ b/solution.py
@@ -43,6 +43,13 @@
     return rows, lane, twist_re, twist_im
 
 
+def lane_dot(x, table):
+    high, low = halves(x)
+    width = table.shape[1] // 2
+    wide = jnp.dot(high, table, preferred_element_type=F32)
+    return wide[:, :width] + (wide[:, width:] + jnp.dot(low, table[:, :width], preferred_element_type=F32))
+
+
 def halves(x):
     high = x.astype(BF16)
     return high, (x - high.astype(F32)).astype(BF16)
@@ -62,7 +69,7 @@
     first = both[:, :lanes] + (both[:, lanes:] + jnp.dot(rows[1], high, preferred_element_type=F32))
     re, im = first[:n], first[n:]
     turned = jnp.concatenate([re * twist_re - im * twist_im, re * twist_im + im * twist_re], axis=1)
-    return dot3(halves(turned), lane)
+    return lane_dot(turned, lane)
 
 
 def fetch(pairs, sems):
@@ -126,12 +133,12 @@
         copy.wait()
 
 
-def spectra_kernel(x_ref, rh, rl, lh, ll, tr, ti, out_ref):
+def spectra_kernel(x_ref, rh, rl, lane, tr, ti, out_ref):
     blocks, both, lanes = x_ref.shape
     chans = both // 2
     for field in range(2):
         x = x_ref[:, field * chans : (field + 1) * chans, :].reshape(blocks * chans, lanes)
-        out_ref[field] = forward(x, (rh[...], rl[...]), (lh[...], ll[...]), tr[...], ti[...])
+        out_ref[field] = forward(x, (rh[...], rl[...]), lane[...], tr[...], ti[...])
 
 
 def far_kernel(far_ref, part_ref, proj_ref, queries_ref, conv_ref, grad_q_ref, grad_ref, turned_ref):
@@ -142,17 +149,17 @@
     grad_q_ref[...] = (total * conv_ref[...].astype(F32)).astype(BF16)
 
 
-def correlate_kernel(scale, stretch, x_ref, spec_ref, rh, rl, lh, ll, rth, rtl, lth, ltl, tr, ti, out_ref):
+def correlate_kernel(scale, stretch, x_ref, spec_ref, rh, rl, lane, rth, rtl, lt, tr, ti, out_ref):
     blocks, chans, lanes = x_ref.shape
     n = blocks * chans
     twist_re, twist_im = tr[...], ti[...]
-    grad = forward(x_ref[...].reshape(n, lanes), (rh[...], rl[...]), (lh[...], ll[...]), twist_re, twist_im)
+    grad = forward(x_ref[...].reshape(n, lanes), (rh[...], rl[...]), lane[...], twist_re, twist_im)
     g_re, g_im = grad[:, :lanes] * scale, grad[:, lanes:] * scale
     sides = []
     for field in range(2):
         s_re, s_im = spec_ref[field, :, :lanes], spec_ref[field, :, lanes:]
         prod = jnp.concatenate([s_re * g_re + s_im * g_im, s_re * g_im - s_im * g_re], axis=1)
-        back = dot3(halves(prod), (lth[...], ltl[...]))
+        back = lane_dot(prod, lt[...])
         re, im = back[:, :lanes], back[:, lanes:]
         sides.append(jnp.concatenate([re * twist_re + im * twist_im, im * twist_re - re * twist_im], axis=0))
     result = dot3((rth[...], rtl[...]), halves(jnp.concatenate(sides, axis=1)))
@@ -205,8 +212,8 @@
     dma = pltpu.SemaphoreType.DMA
 
     rows, lane, twist_re, twist_im = tables(n_ctx, tok, chans)
-    fwd = [jnp.asarray(t) for t in (*split_table(rows), *split_table(lane))]
-    inv = [jnp.asarray(t) for t in (*split_table(rows.T), *split_table(lane.T))]
+    fwd = [jnp.asarray(t) for t in (*split_table(rows), np.concatenate(split_table(lane), axis=1))]
+    inv = [jnp.asarray(t) for t in (*split_table(rows.T), np.concatenate(split_table(lane.T), axis=1))]
     twist = [jnp.asarray(twist_re), jnp.asarray(twist_im)]
     place = jnp.stack([lax.axis_index("zh"), lax.axis_index("core")]).astype(jnp.int32)
 
@@ -226,7 +233,7 @@
         ],
         out_specs=(HBM, VMEM),
     )(long_filter, keys, values, out_grad)
-    far = lax.ppermute(own, "zh", [(0, 1), (1, 0)])
+    far = lax.ppermute(out_grad, "zh", [(0, 1), (1, 0)])
     fields = lax.all_to_all(prepared, CTX, 0, 0)
 
     joined = call(
@@ -249,11 +256,11 @@
     )(across, part, far_proj, gate, saved)
     turned = lax.all_to_all(turned, CTX, 0, 0)
 
-    spec = call(spectra_kernel, shape((2, n_ctx * chans, 2 * tok), F32), [VMEM] * 7)(fields, *fwd, *twist)
+    spec = call(spectra_kernel, shape((2, n_ctx * chans, 2 * tok), F32), [VMEM] * 6)(fields, *fwd, *twist)
     corr = call(
         functools.partial(correlate_kernel, 1.0 / total_len, inv_root * STRETCH),
         shape((n_ctx, 3 * chans, tok), BF16),
-        [VMEM] * 12,
+        [VMEM] * 10,
     )(turned, spec, *fwd, *inv, *twist)
     corr = lax.all_to_all(corr, CTX, 0, 0)
     grad_k, grad_v, filter_grad = call(

time: 96.5 us -> 96.5 us (level)
  transfers between devices with their start and end apart: 4 -> 4, of which waited for: 3 -> 3; matrix products, arithmetic and copies ran while one was open for 0% -> 0% of each run, Pallas kernels for 4% -> 6%
where the time goes in v5:
time: 96.5 us; the launch traced here: 96.1 us
  starting transfers between devices  38 us (39%)
  blocking collectives  34.9 us (36%)
  waiting for transfers between devices  14.1 us (15%)
  Pallas kernels  8.06 us (8%)
    all_to_all x1, blocking collectives, body(): corr = lax.all_to_all(corr, CTX, 0, 0)  21.3 us
    ppermute x1, starting transfers between devices, body(): far = lax.ppermute(out_grad, 'zh', [(0, 1), (1, 0)])  15.7 us
    all_gather x1, blocking collectives, body(): near = lax.all_gather(joined, 'y')  13.7 us
    all_to_all x1, waiting for transfers between devices, body(): turned = lax.all_to_all(turned, CTX, 0, 0)  13.6 us
    all_to_all x1, starting transfers between devices, body(): turned = lax.all_to_all(turned, CTX, 0, 0)  12.5 us
    pallas_call x7, Pallas kernels, call(): return lambda *args: run(*map(held, args, specs))  8.06 us
    all_to_all x1, starting transfers between devices, body(): fields = lax.all_to_all(prepared, CTX, 0, 0)  7.89 us
  transfers between devices with their start and end apart: 4, of which 3 were waited for; matrix products, arithmetic and copies ran while one was open for 0% of the time, Pallas kernels for 6%

profile of v5, /device:TPU:8, one launch (start us, length us, event | category | flops | bytes accessed | tf_op | source)
XLA Modules:
  0.0 96.1 jit_solution(17258159325902581595)
XLA Ops:
  0.6 15.7 %collective-permute-start = (bf16[128,256]{1,0:T(8,128)(2,1)}, bf16[128,256]{1,0:T(8,128)(2,1)S(1)}, u32[]{:S(2)}, u32[]{:S(2)}) collective-permute-start(bf16[128,256]{1,0:T(8,128)(2,1)} %own_hbm.1), channel_id=1, source_target_pairs={{0,8},{8,0},{1,9},{9,1},{2,10},{10,2},{3,11},{11,3},{4,12},{12,4},... | collective-permute-start | bytes 196616 | tf_op jit(solution)/shard_map/ppermute | solution.py:236
  16.4 1.8 %shard_map.183 = (f32[32,16,128]{2,1,0:T(8,128)}, bf16[128,256]{1,0:T(8,128)(2,1)S(1)}) custom-call(f32[128,256]{1,0:T(8,128)} %filter_hbm.1, bf16[128,256]{1,0:T(8,128)(2,1)} %keys_ref.1, bf16[128,256]{1,0:T(8,128)(2,1)} %values_ref.1, bf16[128,256]{1,0:T(8,128)(2,1)} %own_hbm.1), custom_call_target="tpu_custom_call" | custom-call | tf_op jit(solution)/shard_map/pallas_call | solution.py:201
  18.2 7.9 %all-to-all-start.1 = ((f32[32,16,128]{2,1,0:T(8,128)}), f32[32,16,128]{2,1,0:T(8,128)S(1)}, u32[]{:S(2)}, u32[]{:S(2)}) async-start(f32[32,16,128]{2,1,0:T(8,128)} %get-tuple-element.27), calls=%async_computation.1 | async-start | bytes 524288 | tf_op jit(solution)/shard_map/all_to_all | solution.py:237
  26.1 0.1 pad_add_fusion.place_ref
  26.1 0.0 collective-permute-done.far_ref
  26.1 0.6 shard_map.184
  26.7 13.7 %all-gather = bf16[8,128,256]{2,1,0:T(8,128)(2,1)S(1)} all-gather(bf16[2,128,256]{2,1,0:T(8,128)(2,1)S(1)} %shard_map.184), channel_id=2, replica_groups=mesh['x'=4,'zl'=8,'zh'=2,'y'=4,'core'=2] {'y'}, dimensions={0}, use_global_device_ids=true | all-gather | bytes 655360 | tf_op jit(solution)/shard_map/all_gather | solution.py:245
  40.4 1.9 %collective-permute-start.1 = (bf16[4,2,128,256]{3,2,1,0:T(8,128)(2,1)S(1)}, bf16[4,2,128,256]{3,2,1,0:T(8,128)(2,1)S(1)}, u32[]{:S(2)}, u32[]{:S(2)}) collective-permute-start(bf16[4,2,128,256]{3,2,1,0:T(8,128)(2,1)S(1)} %bitcast.6), channel_id=1, source_target_pairs={{0,1},{1,0},{2,3},{3,2},{4,5},{5,4},{6,7},{7,6},{8,9},{9,8},{10,11... | collective-permute-start | bytes 1572872 | tf_op jit(solution)/shard_map/ppermute | solution.py:246
  42.3 0.0 copy-done
  42.3 0.0 copy-start.1
  42.3 0.0 copy-start.2
  42.3 0.0 copy-start.3
  42.3 0.0 copy-start.4
  42.4 0.0 copy-start.5
  42.4 1.4 %shard_map.185 = (f32[128,256]{1,0:T(8,128)S(1)}, bf16[8,256,256]{2,1,0:T(8,128)(2,1)S(1)}, bf16[128,256]{1,0:T(8,128)(2,1)S(1)}, bf16[128,256]{1,0:T(8,128)(2,1)S(1)}) custom-call(s32[2]{0:T(128)S(1)} %pad_add_fusion.place_ref, bf16[4,2,128,256]{3,2,1,0:T(8,128)(2,1)S(1)} %bitcast.7, bf16[8,2,256,256]{3,2,1,0:T(8,128)(2,1)S(1)} %bitcast.5, ...), custom_call_target="tpu_custom_call" | custom-call | tf_op jit(solution)/shard_map/pallas_call | solution.py:201
  43.8 0.0 copy-start.8
  43.8 0.0 copy-start.9
  43.8 0.0 copy-start.10
  43.8 0.3 collective-permute-done.1.far_ref
  44.2 1.0 %shard_map.186 = (bf16[128,256]{1,0:T(8,128)(2,1)}, f32[128,256]{1,0:T(8,128)S(1)}, f32[32,8,128]{2,1,0:T(8,128)}) custom-call(bf16[4,2,128,256]{3,2,1,0:T(8,128)(2,1)S(1)} %collective-permute-done.1.far_ref, f32[128,256]{1,0:T(8,128)S(1)} %get-tuple-element.21.part_ref, bf16[8,256,256]{2,1,0:T(8,128)(2,1)S(1)} %get-tuple-element.22.proj_ref, ...), custom_call_target="tpu_custom_call" | custom-call | tf_op jit(solution)/shard_map/pallas_call | solution.py:201
  45.2 0.1 all-to-all-done.1.x_ref
  45.3 12.5 %all-to-all-start = ((f32[32,8,128]{2,1,0:T(8,128)}), f32[32,8,128]{2,1,0:T(8,128)S(1)}, u32[]{:S(2)}, u32[]{:S(2)}) async-start(f32[32,8,128]{2,1,0:T(8,128)} %get-tuple-element.26), calls=%async_computation | async-start | bytes 262144 | tf_op jit(solution)/shard_map/all_to_all | solution.py:257
  57.9 0.0 copy-start.6
  57.9 0.0 copy-start.7
  57.9 0.0 copy-start.11
  57.9 0.9 shard_map.187.spec_ref
  58.8 13.6 %all-to-all-done.x_ref = f32[32,8,128]{2,1,0:T(8,128)S(1)} async-done(((f32[32,8,128]{2,1,0:T(8,128)}), f32[32,8,128]{2,1,0:T(8,128)S(1)}, u32[]{:S(2)}, u32[]{:S(2)}) %all-to-all-start) | async-done | bytes 131104 | tf_op jit(solution)/shard_map/all_to_all | solution.py:257
  72.5 0.0 copy-done.10
  72.5 1.5 %shard_map.188 = bf16[32,24,128]{2,1,0:T(8,128)(2,1)S(1)} custom-call(f32[32,8,128]{2,1,0:T(8,128)S(1)} %all-to-all-done.x_ref, f32[2,256,256]{2,1,0:T(8,128)S(1)} %shard_map.187.spec_ref, bf16[512,256]{1,0:T(8,128)(2,1)S(1)} %copy-done.1, bf16[512,256]{1,0:T(8,128)(2,1)S(1)} %copy-done.2, bf16[256,512]{1,0:T(8,128)(2,1)S(1)} %copy-done.3, ...), custom_call_target="tpu_custom_call" | custom-call | tf_op jit(solution)/shard_map/pallas_call | solution.py:201
  74.0 21.3 %all_to_all.15.x_ref = bf16[32,24,128]{2,1,0:T(8,128)(2,1)S(1)} all-to-all(bf16[32,24,128]{2,1,0:T(8,128)(2,1)S(1)} %shard_map.188), channel_id=1, replica_groups=mesh['x'=4,'zl'=8,'zh'=2,'y'=4,'core'=2] {'x','zl'}, dimensions={0} | all-to-all | bytes 393216 | tf_op jit(solution)/shard_map/all_to_all | solution.py:265
  95.3 0.0 copy-done.7
  95.3 0.8 shard_map.189
  (10 shorter events, 0.0 us)
Async XLA Ops:
  0.6 25.5 %collective-permute-start = (bf16[128,256]{1,0:T(8,128)(2,1)}, bf16[128,256]{1,0:T(8,128)(2,1)S(1)}, u32[]{:S(2)}, u32[]{:S(2)}) collective-permute-start(bf16[128,256]{1,0:T(8,128)(2,1)} %own_hbm.1), channel_id=1, source_target_pairs={{0,8},{8,0},{1,9},{9,1},{2,10},{10,2},{3,11},{11,3},{4,12},{12,4},... | collective-permute-start | bytes 196616 | tf_op jit(solution)/shard_map/ppermute | solution.py:236
  18.2 27.1 %all-to-all-start.1 = ((f32[32,16,128]{2,1,0:T(8,128)}), f32[32,16,128]{2,1,0:T(8,128)S(1)}, u32[]{:S(2)}, u32[]{:S(2)}) async-start(f32[32,16,128]{2,1,0:T(8,128)} %get-tuple-element.27), calls=%async_computation.1 | async-start | bytes 524288 | tf_op jit(solution)/shard_map/all_to_all | solution.py:237
  26.1 16.2 %copy-start = (bf16[4096,256]{1,0:T(8,128)(2,1)S(1)}, bf16[4096,256]{1,0:T(8,128)(2,1)}, u32[]{:S(2)}) copy-start(bf16[4096,256]{1,0:T(8,128)(2,1)} %param.17) | copy-start | bytes 6291460
  40.4 3.8 %collective-permute-start.1 = (bf16[4,2,128,256]{3,2,1,0:T(8,128)(2,1)S(1)}, bf16[4,2,128,256]{3,2,1,0:T(8,128)(2,1)S(1)}, u32[]{:S(2)}, u32[]{:S(2)}) collective-permute-start(bf16[4,2,128,256]{3,2,1,0:T(8,128)(2,1)S(1)} %bitcast.6), channel_id=1, source_target_pairs={{0,1},{1,0},{2,3},{3,2},{4,5},{5,4},{6,7},{7,6},{8,9},{9,8},{10,11... | collective-permute-start | bytes 1572872 | tf_op jit(solution)/shard_map/ppermute | solution.py:246
  42.3 15.5 %copy-start.1 = (bf16[512,256]{1,0:T(8,128)(2,1)S(1)}, bf16[512,256]{1,0:T(8,128)(2,1)}, u32[]{:S(2)}) copy-start(bf16[512,256]{1,0:T(8,128)(2,1)} %constant.24.clone.rh) | copy-start | bytes 786436
  42.3 15.5 %copy-start.2 = (bf16[512,256]{1,0:T(8,128)(2,1)S(1)}, bf16[512,256]{1,0:T(8,128)(2,1)}, u32[]{:S(2)}) copy-start(bf16[512,256]{1,0:T(8,128)(2,1)} %constant.25.clone.rl) | copy-start | bytes 786436
  42.3 15.5 %copy-start.3 = (bf16[256,512]{1,0:T(8,128)(2,1)S(1)}, bf16[256,512]{1,0:T(8,128)(2,1)}, u32[]{:S(2)}) copy-start(bf16[256,512]{1,0:T(8,128)(2,1)} %constant.26.clone.lane) | copy-start | bytes 786436
  42.3 15.5 %copy-start.4 = (f32[256,128]{1,0:T(8,128)S(1)}, f32[256,128]{1,0:T(8,128)}, u32[]{:S(2)}) copy-start(f32[256,128]{1,0:T(8,128)} %constant.30.clone.tr) | copy-start | bytes 393220
  42.4 15.5 %copy-start.5 = (f32[256,128]{1,0:T(8,128)S(1)}, f32[256,128]{1,0:T(8,128)}, u32[]{:S(2)}) copy-start(f32[256,128]{1,0:T(8,128)} %constant.31.clone.ti) | copy-start | bytes 393220
  43.8 28.6 %copy-start.8 = (bf16[256,512]{1,0:T(8,128)(2,1)S(1)}, bf16[256,512]{1,0:T(8,128)(2,1)}, u32[]{:S(2)}) copy-start(bf16[256,512]{1,0:T(8,128)(2,1)} %constant.27.clone.rth) | copy-start | bytes 786436
  43.8 28.6 %copy-start.9 = (bf16[256,512]{1,0:T(8,128)(2,1)S(1)}, bf16[256,512]{1,0:T(8,128)(2,1)}, u32[]{:S(2)}) copy-start(bf16[256,512]{1,0:T(8,128)(2,1)} %constant.28.clone.rtl) | copy-start | bytes 786436
  43.8 28.6 %copy-start.10 = (bf16[256,512]{1,0:T(8,128)(2,1)S(1)}, bf16[256,512]{1,0:T(8,128)(2,1)}, u32[]{:S(2)}) copy-start(bf16[256,512]{1,0:T(8,128)(2,1)} %constant.29.clone.lt) | copy-start | bytes 786436
  45.3 27.1 %all-to-all-start = ((f32[32,8,128]{2,1,0:T(8,128)}), f32[32,8,128]{2,1,0:T(8,128)S(1)}, u32[]{:S(2)}, u32[]{:S(2)}) async-start(f32[32,8,128]{2,1,0:T(8,128)} %get-tuple-element.26), calls=%async_computation | async-start | bytes 262144 | tf_op jit(solution)/shard_map/all_to_all | solution.py:257
  57.9 37.4 %copy-start.6 = (bf16[128,256]{1,0:T(8,128)(2,1)S(1)}, bf16[128,256]{1,0:T(8,128)(2,1)}, u32[]{:S(2)}) copy-start(bf16[128,256]{1,0:T(8,128)(2,1)} %keys_ref.1) | copy-start | bytes 196612
  57.9 37.4 %copy-start.7 = (bf16[128,256]{1,0:T(8,128)(2,1)S(1)}, bf16[128,256]{1,0:T(8,128)(2,1)}, u32[]{:S(2)}) copy-start(bf16[128,256]{1,0:T(8,128)(2,1)} %values_ref.1) | copy-start | bytes 196612
  57.9 37.4 %copy-start.11 = (f32[256]{0:T(256)S(1)}, f32[256]{0:T(256)}, u32[]{:S(2)}) copy-start(f32[256]{0:T(256)} %param.23) | copy-start | bytes 3076

commit v6 on v4

--- a/solution.py
+++ b/solution.py
@@ -96,12 +96,6 @@
     second.wait()
 
 
-def join_kernel(place_ref, own_ref, far_ref, out_ref):
-    zh = place_ref[0]
-    out_ref[zh] = own_ref[...]
-    out_ref[1 - zh] = far_ref[...]
-
-
 def products(core, given_ref, proj_ref):
     n_y, n_zh = given_ref.shape[:2]
     total = None
@@ -224,17 +218,14 @@
             pltpu.VMEM((tok, width), BF16),
             dma((6,)),
         ],
+        cost=pl.CostEstimate(flops=COST, bytes_accessed=1 << 20, transcendentals=0),
         out_specs=(HBM, VMEM),
     )(long_filter, keys, values, out_grad)
     far = lax.ppermute(own, "zh", [(0, 1), (1, 0)])
     fields = lax.all_to_all(prepared, CTX, 0, 0)
 
-    joined = call(
-        join_kernel,
-        shape((2, tok, width), BF16),
-        [SMEM, VMEM, VMEM],
-        cost=pl.CostEstimate(flops=COST, bytes_accessed=1 << 20, transcendentals=0),
-    )(place, own, far)
+    upper = lax.axis_index("zh") == 1
+    joined = jnp.stack([jnp.where(upper, far, own), jnp.where(upper, own, far)])
     near = lax.all_gather(joined, "y")
     across = lax.ppermute(near, "core", [(0, 1), (1, 0)])
     part, far_proj, gate, saved = call(
@@ -242,6 +233,7 @@
         (shape((tok, width), F32), half, block, block),
         [SMEM, VMEM, VMEM, HBM, HBM],
         [dma((2,))],
+        cost=pl.CostEstimate(flops=COST, bytes_accessed=1 << 20, transcendentals=0),
     )(place, near, proj, queries, conv_out)
     across, part = lax.optimization_barrier((across, part))
     grad_q, grad, turned = call(

time: 96.5 us -> 96 us (level)
    pallas_call x7 -> x6, Pallas kernels: 8.07 us -> 7.67 us  [call(): return lambda *args: run(*map(held, args, specs))]
where the time goes in v6:
time: 96 us; the launch traced here: 95.6 us
  starting transfers between devices  37.3 us (39%)
  blocking collectives  34.9 us (36%)
  waiting for transfers between devices  14.7 us (15%)
  Pallas kernels  7.67 us (8%)
    all_to_all x1, blocking collectives, body(): corr = lax.all_to_all(corr, CTX, 0, 0)  21.3 us
    ppermute x1, starting transfers between devices, body(): far = lax.ppermute(own, 'zh', [(0, 1), (1, 0)])  15.7 us
    all_to_all x1, waiting for transfers between devices, body(): turned = lax.all_to_all(turned, CTX, 0, 0)  13.7 us
    all_gather x1, blocking collectives, body(): near = lax.all_gather(joined, 'y')  13.6 us
    all_to_all x1, starting transfers between devices, body(): turned = lax.all_to_all(turned, CTX, 0, 0)  11.8 us
    all_to_all x1, starting transfers between devices, body(): fields = lax.all_to_all(prepared, CTX, 0, 0)  7.89 us
    pallas_call x6, Pallas kernels, call(): return lambda *args: run(*map(held, args, specs))  7.67 us
  transfers between devices with their start and end apart: 4, of which 3 were waited for; matrix products, arithmetic and copies ran while one was open for 0% of the time, Pallas kernels for 4%

profile of v6, /device:TPU:8, one launch (start us, length us, event | category | flops | bytes accessed | tf_op | source)
XLA Modules:
  0.0 95.6 jit_solution(8859256856866073074)
XLA Ops:
  0.6 1.9 %shard_map.201 = (f32[32,16,128]{2,1,0:T(8,128)}, bf16[128,256]{1,0:T(8,128)(2,1)S(1)}) custom-call(f32[128,256]{1,0:T(8,128)} %filter_hbm.1, bf16[128,256]{1,0:T(8,128)(2,1)} %keys_ref.1, bf16[128,256]{1,0:T(8,128)(2,1)} %values_ref.1, bf16[128,256]{1,0:T(8,128)(2,1)} %own_hbm.1), custom_call_target="tpu_custom_call" | custom-call | flops 34359738368 | bytes 1048576 | tf_op jit(solution)/shard_map/pallas_call | solution.py:188
  2.6 15.7 %collective-permute-start = (bf16[128,256]{1,0:T(8,128)(2,1)S(1)}, bf16[128,256]{1,0:T(8,128)(2,1)S(1)}, u32[]{:S(2)}, u32[]{:S(2)}) collective-permute-start(bf16[128,256]{1,0:T(8,128)(2,1)S(1)} %get-tuple-element.18), channel_id=1, source_target_pairs={{0,8},{8,0},{1,9},{9,1},{2,10},{10,2},{3,11},{11,3},{4,12},{12,4},... | collective-permute-start | bytes 196616 | tf_op jit(solution)/shard_map/ppermute | solution.py:224
  18.3 7.9 %all-to-all-start.1 = ((f32[32,16,128]{2,1,0:T(8,128)}), f32[32,16,128]{2,1,0:T(8,128)S(1)}, u32[]{:S(2)}, u32[]{:S(2)}) async-start(f32[32,16,128]{2,1,0:T(8,128)} %get-tuple-element.27), calls=%async_computation.1 | async-start | bytes 524288 | tf_op jit(solution)/shard_map/all_to_all | solution.py:225
  26.2 0.1 pad_add_fusion.place_ref
  26.3 0.0 collective-permute-done
  26.3 13.6 %all-gather = bf16[8,128,256]{2,1,0:T(8,128)(2,1)S(1)} all-gather(bf16[2,128,256]{2,1,0:T(8,128)(2,1)S(1)} %pad_maximum_fusion), channel_id=2, replica_groups=mesh['x'=4,'zl'=8,'zh'=2,'y'=4,'core'=2] {'y'}, dimensions={0}, use_global_device_ids=true | all-gather | bytes 655360 | tf_op jit(solution)/shard_map/all_gather | solution.py:229
  39.9 1.9 %collective-permute-start.1 = (bf16[4,2,128,256]{3,2,1,0:T(8,128)(2,1)S(1)}, bf16[4,2,128,256]{3,2,1,0:T(8,128)(2,1)S(1)}, u32[]{:S(2)}, u32[]{:S(2)}) collective-permute-start(bf16[4,2,128,256]{3,2,1,0:T(8,128)(2,1)S(1)} %bitcast.9), channel_id=1, source_target_pairs={{0,1},{1,0},{2,3},{3,2},{4,5},{5,4},{6,7},{7,6},{8,9},{9,8},{10,11... | collective-permute-start | bytes 1572872 | tf_op jit(solution)/shard_map/ppermute | solution.py:230
  41.9 1.4 %shard_map.202 = (f32[128,256]{1,0:T(8,128)S(1)}, bf16[8,256,256]{2,1,0:T(8,128)(2,1)S(1)}, bf16[128,256]{1,0:T(8,128)(2,1)S(1)}, bf16[128,256]{1,0:T(8,128)(2,1)S(1)}) custom-call(s32[2]{0:T(128)S(1)} %pad_add_fusion.place_ref, bf16[4,2,128,256]{3,2,1,0:T(8,128)(2,1)S(1)} %bitcast.10, bf16[8,2,256,256]{3,2,1,0:T(8,128)(2,1)S(1)} %bitcast.12, ...), custom_call_target="tpu_custom_call" | custom-call | flops 34359738368 | bytes 1048576 | tf_op jit(solution)/shard_map/pallas_call | solution.py:188
  43.3 0.0 copy-start
  43.3 0.0 copy-start.1
  43.3 0.0 copy-start.2
  43.3 0.0 copy-start.3
  43.4 0.0 copy-start.4
  43.4 0.0 copy-start.5
  43.4 0.0 copy-start.6
  43.4 0.0 copy-start.7
  43.4 0.0 copy-start.8
  43.4 0.0 copy-start.9
  43.4 0.3 collective-permute-done.1.far_ref
  43.7 1.0 %shard_map.203 = (bf16[128,256]{1,0:T(8,128)(2,1)}, f32[128,256]{1,0:T(8,128)S(1)}, f32[32,8,128]{2,1,0:T(8,128)}) custom-call(bf16[4,2,128,256]{3,2,1,0:T(8,128)(2,1)S(1)} %collective-permute-done.1.far_ref, f32[128,256]{1,0:T(8,128)S(1)} %get-tuple-element.21.part_ref, bf16[8,256,256]{2,1,0:T(8,128)(2,1)S(1)} %get-tuple-element.22.proj_ref, ...), custom_call_target="tpu_custom_call" | custom-call | tf_op jit(solution)/shard_map/pallas_call | solution.py:188
  44.8 0.7 all-to-all-done.1.x_ref
  45.5 11.8 %all-to-all-start = ((f32[32,8,128]{2,1,0:T(8,128)}), f32[32,8,128]{2,1,0:T(8,128)S(1)}, u32[]{:S(2)}, u32[]{:S(2)}) async-start(f32[32,8,128]{2,1,0:T(8,128)} %get-tuple-element.26), calls=%async_computation | async-start | bytes 262144 | tf_op jit(solution)/shard_map/all_to_all | solution.py:242
  57.4 0.0 copy-start.10
  57.4 0.0 copy-start.11
  57.4 0.0 copy-start.12
  57.4 0.9 shard_map.204.spec_ref
  58.3 13.7 %all-to-all-done.x_ref = f32[32,8,128]{2,1,0:T(8,128)S(1)} async-done(((f32[32,8,128]{2,1,0:T(8,128)}), f32[32,8,128]{2,1,0:T(8,128)S(1)}, u32[]{:S(2)}, u32[]{:S(2)}) %all-to-all-start) | async-done | bytes 131104 | tf_op jit(solution)/shard_map/all_to_all | solution.py:242
  72.0 0.0 copy-done.8
  72.0 0.0 copy-done.9
  72.0 1.5 %shard_map.205 = bf16[32,24,128]{2,1,0:T(8,128)(2,1)S(1)} custom-call(f32[32,8,128]{2,1,0:T(8,128)S(1)} %all-to-all-done.x_ref, f32[2,256,256]{2,1,0:T(8,128)S(1)} %shard_map.204.spec_ref, bf16[512,256]{1,0:T(8,128)(2,1)S(1)} %copy-done, bf16[512,256]{1,0:T(8,128)(2,1)S(1)} %copy-done.1, bf16[256,256]{1,0:T(8,128)(2,1)S(1)} %copy-done.2, ...), custom_call_target="tpu_custom_call" | custom-call | tf_op jit(solution)/shard_map/pallas_call | solution.py:188
  73.6 21.3 %all_to_all.15.x_ref = bf16[32,24,128]{2,1,0:T(8,128)(2,1)S(1)} all-to-all(bf16[32,24,128]{2,1,0:T(8,128)(2,1)S(1)} %shard_map.205), channel_id=1, replica_groups=mesh['x'=4,'zl'=8,'zh'=2,'y'=4,'core'=2] {'x','zl'}, dimensions={0} | all-to-all | bytes 393216 | tf_op jit(solution)/shard_map/all_to_all | solution.py:250
  94.8 0.8 shard_map.206
  (15 shorter events, 0.1 us)
Async XLA Ops:
  0.6 41.2 %copy-start.13 = (bf16[4096,256]{1,0:T(8,128)(2,1)S(1)}, bf16[4096,256]{1,0:T(8,128)(2,1)}, u32[]{:S(2)}) copy-start(bf16[4096,256]{1,0:T(8,128)(2,1)} %param.19) | copy-start | bytes 6291460
  2.6 23.7 %collective-permute-start = (bf16[128,256]{1,0:T(8,128)(2,1)S(1)}, bf16[128,256]{1,0:T(8,128)(2,1)S(1)}, u32[]{:S(2)}, u32[]{:S(2)}) collective-permute-start(bf16[128,256]{1,0:T(8,128)(2,1)S(1)} %get-tuple-element.18), channel_id=1, source_target_pairs={{0,8},{8,0},{1,9},{9,1},{2,10},{10,2},{3,11},{11,3},{4,12},{12,4},... | collective-permute-start | bytes 196616 | tf_op jit(solution)/shard_map/ppermute | solution.py:224
  18.3 27.1 %all-to-all-start.1 = ((f32[32,16,128]{2,1,0:T(8,128)}), f32[32,16,128]{2,1,0:T(8,128)S(1)}, u32[]{:S(2)}, u32[]{:S(2)}) async-start(f32[32,16,128]{2,1,0:T(8,128)} %get-tuple-element.27), calls=%async_computation.1 | async-start | bytes 524288 | tf_op jit(solution)/shard_map/all_to_all | solution.py:225
  39.9 3.8 %collective-permute-start.1 = (bf16[4,2,128,256]{3,2,1,0:T(8,128)(2,1)S(1)}, bf16[4,2,128,256]{3,2,1,0:T(8,128)(2,1)S(1)}, u32[]{:S(2)}, u32[]{:S(2)}) collective-permute-start(bf16[4,2,128,256]{3,2,1,0:T(8,128)(2,1)S(1)} %bitcast.9), channel_id=1, source_target_pairs={{0,1},{1,0},{2,3},{3,2},{4,5},{5,4},{6,7},{7,6},{8,9},{9,8},{10,11... | collective-permute-start | bytes 1572872 | tf_op jit(solution)/shard_map/ppermute | solution.py:230
  43.3 14.0 %copy-start = (bf16[512,256]{1,0:T(8,128)(2,1)S(1)}, bf16[512,256]{1,0:T(8,128)(2,1)}, u32[]{:S(2)}) copy-start(bf16[512,256]{1,0:T(8,128)(2,1)} %constant.30.clone.rh) | copy-start | bytes 786436
  43.3 14.0 %copy-start.1 = (bf16[512,256]{1,0:T(8,128)(2,1)S(1)}, bf16[512,256]{1,0:T(8,128)(2,1)}, u32[]{:S(2)}) copy-start(bf16[512,256]{1,0:T(8,128)(2,1)} %constant.31.clone.rl) | copy-start | bytes 786436
  43.3 14.0 %copy-start.2 = (bf16[256,256]{1,0:T(8,128)(2,1)S(1)}, bf16[256,256]{1,0:T(8,128)(2,1)}, u32[]{:S(2)}) copy-start(bf16[256,256]{1,0:T(8,128)(2,1)} %constant.32.clone.lh) | copy-start | bytes 393220
  43.3 14.0 %copy-start.3 = (bf16[256,256]{1,0:T(8,128)(2,1)S(1)}, bf16[256,256]{1,0:T(8,128)(2,1)}, u32[]{:S(2)}) copy-start(bf16[256,256]{1,0:T(8,128)(2,1)} %constant.33.clone.ll) | copy-start | bytes 393220
  43.4 14.0 %copy-start.4 = (f32[256,128]{1,0:T(8,128)S(1)}, f32[256,128]{1,0:T(8,128)}, u32[]{:S(2)}) copy-start(f32[256,128]{1,0:T(8,128)} %constant.38.clone.tr) | copy-start | bytes 393220
  43.4 14.0 %copy-start.5 = (f32[256,128]{1,0:T(8,128)S(1)}, f32[256,128]{1,0:T(8,128)}, u32[]{:S(2)}) copy-start(f32[256,128]{1,0:T(8,128)} %constant.39.clone.ti) | copy-start | bytes 393220
  43.4 28.6 %copy-start.6 = (bf16[256,512]{1,0:T(8,128)(2,1)S(1)}, bf16[256,512]{1,0:T(8,128)(2,1)}, u32[]{:S(2)}) copy-start(bf16[256,512]{1,0:T(8,128)(2,1)} %constant.34.clone.rth) | copy-start | bytes 786436
  43.4 28.6 %copy-start.7 = (bf16[256,512]{1,0:T(8,128)(2,1)S(1)}, bf16[256,512]{1,0:T(8,128)(2,1)}, u32[]{:S(2)}) copy-start(bf16[256,512]{1,0:T(8,128)(2,1)} %constant.35.clone.rtl) | copy-start | bytes 786436
  43.4 28.6 %copy-start.8 = (bf16[256,256]{1,0:T(8,128)(2,1)S(1)}, bf16[256,256]{1,0:T(8,128)(2,1)}, u32[]{:S(2)}) copy-start(bf16[256,256]{1,0:T(8,128)(2,1)} %constant.36.clone.lth) | copy-start | bytes 393220
  43.4 28.6 %copy-start.9 = (bf16[256,256]{1,0:T(8,128)(2,1)S(1)}, bf16[256,256]{1,0:T(8,128)(2,1)}, u32[]{:S(2)}) copy-start(bf16[256,256]{1,0:T(8,128)(2,1)} %constant.37.clone.ltl) | copy-start | bytes 393220
  45.5 26.5 %all-to-all-start = ((f32[32,8,128]{2,1,0:T(8,128)}), f32[32,8,128]{2,1,0:T(8,128)S(1)}, u32[]{:S(2)}, u32[]{:S(2)}) async-start(f32[32,8,128]{2,1,0:T(8,128)} %get-tuple-element.26), calls=%async_computation | async-start | bytes 262144 | tf_op jit(solution)/shard_map/all_to_all | solution.py:242
  57.4 37.5 %copy-start.10 = (bf16[128,256]{1,0:T(8,128)(2,1)S(1)}, bf16[128,256]{1,0:T(8,128)(2,1)}, u32[]{:S(2)}) copy-start(bf16[128,256]{1,0:T(8,128)(2,1)} %keys_ref.1) | copy-start | bytes 196612
  57.4 37.4 %copy-start.11 = (bf16[128,256]{1,0:T(8,128)(2,1)S(1)}, bf16[128,256]{1,0:T(8,128)(2,1)}, u32[]{:S(2)}) copy-start(bf16[128,256]{1,0:T(8,128)(2,1)} %values_ref.1) | copy-start | bytes 196612
  57.4 37.4 %copy-start.12 = (f32[256]{0:T(256)S(1)}, f32[256]{0:T(256)}, u32[]{:S(2)}) copy-start(f32[256]{0:T(256)} %param.25) | copy-start | bytes 3076

commit v7 on v6

--- a/solution.py
+++ b/solution.py
@@ -221,7 +221,7 @@
         cost=pl.CostEstimate(flops=COST, bytes_accessed=1 << 20, transcendentals=0),
         out_specs=(HBM, VMEM),
     )(long_filter, keys, values, out_grad)
-    far = lax.ppermute(own, "zh", [(0, 1), (1, 0)])
+    far = lax.ppermute(out_grad, "zh", [(0, 1), (1, 0)])
     fields = lax.all_to_all(prepared, CTX, 0, 0)
 
     upper = lax.axis_index("zh") == 1

time: 96 us -> 96 us (level)
  transfers between devices with their start and end apart: 4 -> 4, of which waited for: 3 -> 3; matrix products, arithmetic and copies ran while one was open for 0% -> 0% of each run, Pallas kernels for 4% -> 5%
where the time goes in v7:
time: 96 us; the launch traced here: 95.6 us
  starting transfers between devices  37.5 us (39%)
  blocking collectives  34.9 us (36%)
  waiting for transfers between devices  14.7 us (15%)
  Pallas kernels  7.52 us (8%)
    all_to_all x1, blocking collectives, body(): corr = lax.all_to_all(corr, CTX, 0, 0)  21.3 us
    ppermute x1, starting transfers between devices, body(): far = lax.ppermute(out_grad, 'zh', [(0, 1), (1, 0)])  15.9 us
    all_to_all x1, waiting for transfers between devices, body(): turned = lax.all_to_all(turned, CTX, 0, 0)  13.7 us
    all_gather x1, blocking collectives, body(): near = lax.all_gather(joined, 'y')  13.6 us
    all_to_all x1, starting transfers between devices, body(): turned = lax.all_to_all(turned, CTX, 0, 0)  11.8 us
    all_to_all x1, starting transfers between devices, body(): fields = lax.all_to_all(prepared, CTX, 0, 0)  7.88 us
    pallas_call x6, Pallas kernels, call(): return lambda *args: run(*map(held, args, specs))  7.52 us
  transfers between devices with their start and end apart: 4, of which 3 were waited for; matrix products, arithmetic and copies ran while one was open for 0% of the time, Pallas kernels for 5%

profile of v7, /device:TPU:8, one launch (start us, length us, event | category | flops | bytes accessed | tf_op | source)
XLA Modules:
  0.0 95.6 jit_solution(9977387727403339055)
XLA Ops:
  0.6 0.0 copy-start.13
  0.6 15.9 %collective-permute-start = (bf16[128,256]{1,0:T(8,128)(2,1)}, bf16[128,256]{1,0:T(8,128)(2,1)S(1)}, u32[]{:S(2)}, u32[]{:S(2)}) collective-permute-start(bf16[128,256]{1,0:T(8,128)(2,1)} %own_hbm.1), channel_id=1, source_target_pairs={{0,8},{8,0},{1,9},{9,1},{2,10},{10,2},{3,11},{11,3},{4,12},{12,4},... | collective-permute-start | bytes 196616 | tf_op jit(solution)/shard_map/ppermute | solution.py:224
  16.5 1.8 %shard_map.201 = (f32[32,16,128]{2,1,0:T(8,128)}, bf16[128,256]{1,0:T(8,128)(2,1)S(1)}) custom-call(f32[128,256]{1,0:T(8,128)} %filter_hbm.1, bf16[128,256]{1,0:T(8,128)(2,1)} %keys_ref.1, bf16[128,256]{1,0:T(8,128)(2,1)} %values_ref.1, bf16[128,256]{1,0:T(8,128)(2,1)} %own_hbm.1), custom_call_target="tpu_custom_call" | custom-call | flops 34359738368 | bytes 1048576 | tf_op jit(solution)/shard_map/pallas_call | solution.py:188
  18.3 7.9 %all-to-all-start.1 = ((f32[32,16,128]{2,1,0:T(8,128)}), f32[32,16,128]{2,1,0:T(8,128)S(1)}, u32[]{:S(2)}, u32[]{:S(2)}) async-start(f32[32,16,128]{2,1,0:T(8,128)} %get-tuple-element.27), calls=%async_computation.1 | async-start | bytes 524288 | tf_op jit(solution)/shard_map/all_to_all | solution.py:225
  26.2 0.1 pad_add_fusion.place_ref
  26.3 0.0 collective-permute-done
  26.3 13.6 %all-gather = bf16[8,128,256]{2,1,0:T(8,128)(2,1)S(1)} all-gather(bf16[2,128,256]{2,1,0:T(8,128)(2,1)S(1)} %pad_maximum_fusion), channel_id=2, replica_groups=mesh['x'=4,'zl'=8,'zh'=2,'y'=4,'core'=2] {'y'}, dimensions={0}, use_global_device_ids=true | all-gather | bytes 655360 | tf_op jit(solution)/shard_map/all_gather | solution.py:229
  39.9 1.9 %collective-permute-start.1 = (bf16[4,2,128,256]{3,2,1,0:T(8,128)(2,1)S(1)}, bf16[4,2,128,256]{3,2,1,0:T(8,128)(2,1)S(1)}, u32[]{:S(2)}, u32[]{:S(2)}) collective-permute-start(bf16[4,2,128,256]{3,2,1,0:T(8,128)(2,1)S(1)} %bitcast.9), channel_id=1, source_target_pairs={{0,1},{1,0},{2,3},{3,2},{4,5},{5,4},{6,7},{7,6},{8,9},{9,8},{10,11... | collective-permute-start | bytes 1572872 | tf_op jit(solution)/shard_map/ppermute | solution.py:230
  41.8 1.4 %shard_map.202 = (f32[128,256]{1,0:T(8,128)S(1)}, bf16[8,256,256]{2,1,0:T(8,128)(2,1)S(1)}, bf16[128,256]{1,0:T(8,128)(2,1)S(1)}, bf16[128,256]{1,0:T(8,128)(2,1)S(1)}) custom-call(s32[2]{0:T(128)S(1)} %pad_add_fusion.place_ref, bf16[4,2,128,256]{3,2,1,0:T(8,128)(2,1)S(1)} %bitcast.10, bf16[8,2,256,256]{3,2,1,0:T(8,128)(2,1)S(1)} %bitcast.12, ...), custom_call_target="tpu_custom_call" | custom-call | flops 34359738368 | bytes 1048576 | tf_op jit(solution)/shard_map/pallas_call | solution.py:188
  43.3 0.0 copy-start
  43.3 0.0 copy-start.1
  43.3 0.0 copy-start.2
  43.3 0.0 copy-start.3
  43.3 0.0 copy-start.4
  43.4 0.0 copy-start.5
  43.4 0.0 copy-start.6
  43.4 0.0 copy-start.7
  43.4 0.0 copy-start.8
  43.4 0.0 copy-start.9
  43.4 0.3 collective-permute-done.1.far_ref
  43.7 1.0 %shard_map.203 = (bf16[128,256]{1,0:T(8,128)(2,1)}, f32[128,256]{1,0:T(8,128)S(1)}, f32[32,8,128]{2,1,0:T(8,128)}) custom-call(bf16[4,2,128,256]{3,2,1,0:T(8,128)(2,1)S(1)} %collective-permute-done.1.far_ref, f32[128,256]{1,0:T(8,128)S(1)} %get-tuple-element.21.part_ref, bf16[8,256,256]{2,1,0:T(8,128)(2,1)S(1)} %get-tuple-element.22.proj_ref, ...), custom_call_target="tpu_custom_call" | custom-call | tf_op jit(solution)/shard_map/pallas_call | solution.py:188
  44.7 0.7 all-to-all-done.1.x_ref
  45.4 11.8 %all-to-all-start = ((f32[32,8,128]{2,1,0:T(8,128)}), f32[32,8,128]{2,1,0:T(8,128)S(1)}, u32[]{:S(2)}, u32[]{:S(2)}) async-start(f32[32,8,128]{2,1,0:T(8,128)} %get-tuple-element.26), calls=%async_computation | async-start | bytes 262144 | tf_op jit(solution)/shard_map/all_to_all | solution.py:242
  57.3 0.0 copy-start.10
  57.4 0.0 copy-start.11
  57.4 0.0 copy-start.12
  57.4 0.9 shard_map.204.spec_ref
  58.3 13.7 %all-to-all-done.x_ref = f32[32,8,128]{2,1,0:T(8,128)S(1)} async-done(((f32[32,8,128]{2,1,0:T(8,128)}), f32[32,8,128]{2,1,0:T(8,128)S(1)}, u32[]{:S(2)}, u32[]{:S(2)}) %all-to-all-start) | async-done | bytes 131104 | tf_op jit(solution)/shard_map/all_to_all | solution.py:242
  72.0 0.0 copy-done.9
  72.0 1.5 %shard_map.205 = bf16[32,24,128]{2,1,0:T(8,128)(2,1)S(1)} custom-call(f32[32,8,128]{2,1,0:T(8,128)S(1)} %all-to-all-done.x_ref, f32[2,256,256]{2,1,0:T(8,128)S(1)} %shard_map.204.spec_ref, bf16[512,256]{1,0:T(8,128)(2,1)S(1)} %copy-done, bf16[512,256]{1,0:T(8,128)(2,1)S(1)} %copy-done.1, bf16[256,256]{1,0:T(8,128)(2,1)S(1)} %copy-done.2, ...), custom_call_target="tpu_custom_call" | custom-call | tf_op jit(solution)/shard_map/pallas_call | solution.py:188
  73.5 21.3 %all_to_all.15.x_ref = bf16[32,24,128]{2,1,0:T(8,128)(2,1)S(1)} all-to-all(bf16[32,24,128]{2,1,0:T(8,128)(2,1)S(1)} %shard_map.205), channel_id=1, replica_groups=mesh['x'=4,'zl'=8,'zh'=2,'y'=4,'core'=2] {'x','zl'}, dimensions={0} | all-to-all | bytes 393216 | tf_op jit(solution)/shard_map/all_to_all | solution.py:250
  94.8 0.8 shard_map.206
  (15 shorter events, 0.1 us)
Async XLA Ops:
  0.6 41.2 %copy-start.13 = (bf16[4096,256]{1,0:T(8,128)(2,1)S(1)}, bf16[4096,256]{1,0:T(8,128)(2,1)}, u32[]{:S(2)}) copy-start(bf16[4096,256]{1,0:T(8,128)(2,1)} %param.19) | copy-start | bytes 6291460
  0.6 25.6 %collective-permute-start = (bf16[128,256]{1,0:T(8,128)(2,1)}, bf16[128,256]{1,0:T(8,128)(2,1)S(1)}, u32[]{:S(2)}, u32[]{:S(2)}) collective-permute-start(bf16[128,256]{1,0:T(8,128)(2,1)} %own_hbm.1), channel_id=1, source_target_pairs={{0,8},{8,0},{1,9},{9,1},{2,10},{10,2},{3,11},{11,3},{4,12},{12,4},... | collective-permute-start | bytes 196616 | tf_op jit(solution)/shard_map/ppermute | solution.py:224
  18.3 27.1 %all-to-all-start.1 = ((f32[32,16,128]{2,1,0:T(8,128)}), f32[32,16,128]{2,1,0:T(8,128)S(1)}, u32[]{:S(2)}, u32[]{:S(2)}) async-start(f32[32,16,128]{2,1,0:T(8,128)} %get-tuple-element.27), calls=%async_computation.1 | async-start | bytes 524288 | tf_op jit(solution)/shard_map/all_to_all | solution.py:225
  39.9 3.8 %collective-permute-start.1 = (bf16[4,2,128,256]{3,2,1,0:T(8,128)(2,1)S(1)}, bf16[4,2,128,256]{3,2,1,0:T(8,128)(2,1)S(1)}, u32[]{:S(2)}, u32[]{:S(2)}) collective-permute-start(bf16[4,2,128,256]{3,2,1,0:T(8,128)(2,1)S(1)} %bitcast.9), channel_id=1, source_target_pairs={{0,1},{1,0},{2,3},{3,2},{4,5},{5,4},{6,7},{7,6},{8,9},{9,8},{10,11... | collective-permute-start | bytes 1572872 | tf_op jit(solution)/shard_map/ppermute | solution.py:230
  43.3 14.0 %copy-start = (bf16[512,256]{1,0:T(8,128)(2,1)S(1)}, bf16[512,256]{1,0:T(8,128)(2,1)}, u32[]{:S(2)}) copy-start(bf16[512,256]{1,0:T(8,128)(2,1)} %constant.30.clone.rh) | copy-start | bytes 786436
  43.3 14.0 %copy-start.1 = (bf16[512,256]{1,0:T(8,128)(2,1)S(1)}, bf16[512,256]{1,0:T(8,128)(2,1)}, u32[]{:S(2)}) copy-start(bf16[512,256]{1,0:T(8,128)(2,1)} %constant.31.clone.rl) | copy-start | bytes 786436
  43.3 14.0 %copy-start.2 = (bf16[256,256]{1,0:T(8,128)(2,1)S(1)}, bf16[256,256]{1,0:T(8,128)(2,1)}, u32[]{:S(2)}) copy-start(bf16[256,256]{1,0:T(8,128)(2,1)} %constant.32.clone.lh) | copy-start | bytes 393220
  43.3 14.0 %copy-start.3 = (bf16[256,256]{1,0:T(8,128)(2,1)S(1)}, bf16[256,256]{1,0:T(8,128)(2,1)}, u32[]{:S(2)}) copy-start(bf16[256,256]{1,0:T(8,128)(2,1)} %constant.33.clone.ll) | copy-start | bytes 393220
  43.3 14.0 %copy-start.4 = (f32[256,128]{1,0:T(8,128)S(1)}, f32[256,128]{1,0:T(8,128)}, u32[]{:S(2)}) copy-start(f32[256,128]{1,0:T(8,128)} %constant.38.clone.tr) | copy-start | bytes 393220
  43.4 14.0 %copy-start.5 = (f32[256,128]{1,0:T(8,128)S(1)}, f32[256,128]{1,0:T(8,128)}, u32[]{:S(2)}) copy-start(f32[256,128]{1,0:T(8,128)} %constant.39.clone.ti) | copy-start | bytes 393220
  43.4 28.6 %copy-start.6 = (bf16[256,512]{1,0:T(8,128)(2,1)S(1)}, bf16[256,512]{1,0:T(8,128)(2,1)}, u32[]{:S(2)}) copy-start(bf16[256,512]{1,0:T(8,128)(2,1)} %constant.34.clone.rth) | copy-start | bytes 786436
  43.4 28.6 %copy-start.7 = (bf16[256,512]{1,0:T(8,128)(2,1)S(1)}, bf16[256,512]{1,0:T(8,128)(2,1)}, u32[]{:S(2)}) copy-start(bf16[256,512]{1,0:T(8,128)(2,1)} %constant.35.clone.rtl) | copy-start | bytes 786436
  43.4 28.6 %copy-start.8 = (bf16[256,256]{1,0:T(8,128)(2,1)S(1)}, bf16[256,256]{1,0:T(8,128)(2,1)}, u32[]{:S(2)}) copy-start(bf16[256,256]{1,0:T(8,128)(2,1)} %constant.36.clone.lth) | copy-start | bytes 393220
  43.4 28.6 %copy-start.9 = (bf16[256,256]{1,0:T(8,128)(2,1)S(1)}, bf16[256,256]{1,0:T(8,128)(2,1)}, u32[]{:S(2)}) copy-start(bf16[256,256]{1,0:T(8,128)(2,1)} %constant.37.clone.ltl) | copy-start | bytes 393220
  45.4 26.5 %all-to-all-start = ((f32[32,8,128]{2,1,0:T(8,128)}), f32[32,8,128]{2,1,0:T(8,128)S(1)}, u32[]{:S(2)}, u32[]{:S(2)}) async-start(f32[32,8,128]{2,1,0:T(8,128)} %get-tuple-element.26), calls=%async_computation | async-start | bytes 262144 | tf_op jit(solution)/shard_map/all_to_all | solution.py:242
  57.3 37.5 %copy-start.10 = (bf16[128,256]{1,0:T(8,128)(2,1)S(1)}, bf16[128,256]{1,0:T(8,128)(2,1)}, u32[]{:S(2)}) copy-start(bf16[128,256]{1,0:T(8,128)(2,1)} %keys_ref.1) | copy-start | bytes 196612
  57.4 37.4 %copy-start.11 = (bf16[128,256]{1,0:T(8,128)(2,1)S(1)}, bf16[128,256]{1,0:T(8,128)(2,1)}, u32[]{:S(2)}) copy-start(bf16[128,256]{1,0:T(8,128)(2,1)} %values_ref.1) | copy-start | bytes 196612
  57.4 37.4 %copy-start.12 = (f32[256]{0:T(256)S(1)}, f32[256]{0:T(256)}, u32[]{:S(2)}) copy-start(f32[256]{0:T(256)} %param.25) | copy-start | bytes 3076
